TPU v7x, 256 devices: a whole 4x4x8 slice. The times are simulated.
256 devices in a mesh: ep: 64 (over z_lo, y, x), dp: 4 (over z_hi, core).
Axes of the slice: x: 4, y: 4, z: 8 (z_hi: 2, z_lo: 4; z = z_hi * 4 + z_lo), core: 2. Of those that a mesh axis runs over, the one named last changes fastest.
Arguments:
- tokens: bfloat16 [32768, 1792], P(('ep', 'dp')), may hold values from -6 to 6
- cotangent: bfloat16 [32768, 1792], P(('ep', 'dp')), may hold values from -6 to 6
- slot_choice: int32 [32768, 2], P(('ep', 'dp')), may hold values from 0 to 63, all different within a row; in each aligned block of 128 rows (0 to 127, 128 to 255, ...) at most 5 rows name the same one
- gate_values: float32 [32768, 2], P(('ep', 'dp')), may hold values from 0.1 to 1
- slot_expert: int32 [64], replicated, may hold values from 0 to 31, as said below
- gate_weight: bfloat16 [64, 1792, 1280], P('ep', None, 'dp'), as said below
- up_weight: bfloat16 [64, 1792, 1280], P('ep', None, 'dp'), as said below
- down_weight: bfloat16 [64, 1280, 1792], P('ep', 'dp'), as said below
Outputs:
- token_grad: bfloat16 [32768, 1792], P(('ep', 'dp'))
- down_grad: bfloat16 [64, 1280, 1792], P('ep', 'dp')
Inputs may be any that keep to these rules, and one draw needn't show every extreme that they name: `slot_choice`: each row names 2 different slots; among the rows of one device no slot is named more than 5 times, a bound that some block reaches. `slot_expert`: every expert is held by at least one slot. `gate_weight`: slots that hold the same expert have equal matrices. `up_weight`: slots that hold the same expert have equal matrices. `down_weight`: slots that hold the same expert have equal matrices.
All inputs are finite; a program needn't handle non-finite values.
Results may differ from a plain program's by a relative error of at most 0.0098.
Values may be sent and summed in bfloat16 or wider, within the bound.
No kernel may reach another device: no remote copies, remote signals or barrier semaphores. Data moves between devices by JAX's collectives and lax.ppermute only.
A program may use at most 128 MiB of HBM per device.

v0:
```python
import jax
import jax.numpy as jnp
from jax import lax
from jax.sharding import PartitionSpec as P


def in_blocks(array, dim, count):
    lengths = array.shape
    parts = array.reshape(*lengths[:dim], count, lengths[dim] // count, *lengths[dim + 1 :])
    return jnp.moveaxis(parts, dim, 0)


def cut_rows(length, count):
    unit = 8 if length >= 8 * count else 1
    return [length // unit * k // count * unit for k in range(1, count)]


def joined_along(parts, dim):
    parts = jnp.moveaxis(parts, 0, dim)
    lengths = parts.shape
    return parts.reshape(*lengths[:dim], lengths[dim] * lengths[dim + 1], *lengths[dim + 2 :])


def several_exchanges(array, axis, pieces, split_dim, concat_dim):
    parts = in_blocks(array, split_dim, lax.axis_size(axis))
    split_at = max(range(1, max(2, parts.ndim - 1)), key=lambda d: parts.shape[d])
    gathered = []
    for section in jnp.split(parts, cut_rows(parts.shape[split_at], pieces), axis=split_at):
        if section.size:
            gathered.append(lax.all_to_all(section, axis, split_axis=0, concat_axis=0, tiled=True))
    return joined_along(jnp.concatenate(gathered, axis=split_at), concat_dim)


def per_device(
    tokens, cotangent, slot_choice, gate_values, slot_expert, gate_weight, up_weight, down_weight
):
    n_slots = lax.axis_size("ep")
    tok_rows, width = tokens.shape
    topk = slot_choice.shape[1]
    capacity = max(2, 5 * tok_rows * topk // (4 * n_slots))
    rows_out = n_slots * capacity
    flat_slot = slot_choice.reshape(-1)
    onehot = (flat_slot[:, None] == jnp.arange(n_slots, dtype=jnp.int32)[None, :]).astype(jnp.int32)
    position = jnp.sum(jnp.cumsum(onehot, axis=0) * onehot, axis=1) - 1
    dest = flat_slot * capacity + position
    target = (dest[None, :] == jnp.arange(rows_out, dtype=jnp.int32)[:, None]).reshape(
        rows_out, tok_rows, topk
    )
    select = jnp.any(target, axis=2).astype(jnp.bfloat16)
    weight_table = jnp.sum(jnp.where(target, gate_values[None, :, :], 0.0), axis=2)
    sent_x = jnp.dot(select, tokens, preferred_element_type=jnp.float32).astype(jnp.bfloat16)
    sent_g = jnp.dot(
        weight_table,
        cotangent.astype(jnp.float32),
        precision=lax.Precision.HIGHEST,
        preferred_element_type=jnp.float32,
    ).astype(jnp.bfloat16)
    sent_x = sent_x.reshape(n_slots, capacity, width)
    sent_g = sent_g.reshape(n_slots, capacity, width)
    recv_x, recv_g = (
        lax.all_to_all(sent_x, "ep", split_axis=0, concat_axis=0, tiled=True),
        lax.all_to_all(sent_g, "ep", split_axis=0, concat_axis=0, tiled=True),
    )
    all_x, all_g = (
        lax.all_gather(recv_x, "dp", axis=0, tiled=True),
        lax.all_gather(recv_g, "dp", axis=0, tiled=True),
    )
    groups = all_x.shape[0] // n_slots
    rows_x = all_x.reshape(-1, width)
    rows_g = all_g.reshape(-1, width)
    w_gate = gate_weight[0]
    w_up = up_weight[0]
    w_down = down_weight[0]
    gate = jnp.dot(rows_x, w_gate, preferred_element_type=jnp.float32)
    up = jnp.dot(rows_x, w_up, preferred_element_type=jnp.float32)
    sig = jax.nn.sigmoid(gate)
    act = (gate * sig * up).astype(jnp.bfloat16)
    d_act = lax.dot_general(
        rows_g, w_down, (((1,), (1,)), ((), ())), preferred_element_type=jnp.float32
    )
    d_gate = (d_act * up * sig * (1.0 + gate * (1.0 - sig))).astype(jnp.bfloat16)
    d_up = (d_act * gate * sig).astype(jnp.bfloat16)
    partial_value = lax.dot_general(
        d_gate, w_gate, (((1,), (1,)), ((), ())), preferred_element_type=jnp.float32
    )
    partial_value = partial_value + lax.dot_general(
        d_up, w_up, (((1,), (1,)), ((), ())), preferred_element_type=jnp.float32
    )
    partial_value = partial_value.reshape(groups, n_slots, capacity, width)
    summed = lax.psum_scatter(
        partial_value.astype(jnp.bfloat16), "dp", scatter_dimension=0, tiled=True
    )
    back = lax.all_to_all(summed, "ep", split_axis=1, concat_axis=1, tiled=True)
    back = back.reshape(rows_out, width)
    token_grad = lax.dot_general(
        select, back, (((0,), (0,)), ((), ())), preferred_element_type=jnp.float32
    )
    slot_grad = lax.dot_general(
        act, rows_g, (((0,), (0,)), ((), ())), preferred_element_type=jnp.float32
    )
    hidden = slot_grad.shape[0]
    pieces = slot_grad.reshape(n_slots, -1)
    received = lax.all_to_all(
        pieces.astype(jnp.bfloat16), "ep", split_axis=0, concat_axis=0, tiled=True
    ).astype(pieces.dtype)
    same = (slot_expert[:, None] == slot_expert[None, :]).astype(jnp.float32)
    combined = jnp.dot(
        same, received, precision=lax.Precision.HIGHEST, preferred_element_type=jnp.float32
    )
    returned = several_exchanges(combined.astype(jnp.bfloat16), "ep", 2, 0, 0).astype(
        combined.dtype
    )
    down_grad = returned.reshape(1, hidden, width).astype(jnp.bfloat16)
    return (token_grad.astype(jnp.bfloat16), down_grad)


def solution(mesh):
    return jax.shard_map(
        per_device,
        mesh=mesh,
        in_specs=(
            P(("ep", "dp"), None),
            P(("ep", "dp"), None),
            P(("ep", "dp"), None),
            P(("ep", "dp"), None),
            P(),
            P("ep", None, "dp"),
            P("ep", None, "dp"),
            P("ep", "dp", None),
        ),
        out_specs=(P(("ep", "dp"), None), P("ep", "dp", None)),
        check_vma=False,
    )
```

profile of v0, /device:TPU:2, one launch (start us, length us, event | category | flops | bytes accessed | tf_op | source)
XLA Modules:
  0.0 522.4 jit_solution(6707591645249095951)
XLA Ops:
  10.3 2.5 convolution_convert_fusion.1
  15.1 56.4 %all_to_all.29 = bf16[64,5,1792]{2,1,0:T(8,128)(2,1)S(1)} all-to-all(bf16[64,5,1792]{2,1,0:T(8,128)(2,1)S(1)} %reshape.90), channel_id=1, replica_groups=mesh['ep'=64,'dp'=4] {'ep'}, dimensions={0} | all-to-all | bytes 2293760 | tf_op jit(solution)/shard_map/all_to_all | solution.py:61
  77.2 98.8 %all_to_all.30 = bf16[64,5,1792]{2,1,0:T(8,128)(2,1)S(1)} all-to-all(bf16[64,5,1792]{2,1,0:T(8,128)(2,1)S(1)} %reshape.88), channel_id=1, replica_groups=mesh['ep'=64,'dp'=4] {'ep'}, dimensions={0} | all-to-all | bytes 2293760 | tf_op jit(solution)/shard_map/all_to_all | solution.py:62
  177.8 8.1 %copy.64 = bf16[256,5,1792]{2,1,0:T(8,128)(2,1)} copy(bf16[256,5,1792]{2,0,1:T(8,128)(2,1)} %all-gather.5.cloned.1.call-done) | data formatting | bytes 9175040 | tf_op jit(solution)/shard_map/all_gather | solution.py:65
  185.9 9.7 %reshape.91 = bf16[1280,1792]{1,0:T(8,128)(2,1)} reshape(bf16[256,5,1792]{2,1,0:T(8,128)(2,1)} %copy.64) | data formatting | bytes 9175040 | tf_op jit(solution)/shard_map/reshape | solution.py:69
  195.5 4.1 fusion.6
  199.7 2.8 fusion.9
  202.6 42.7 %all-gather.3.cloned.1.call-done = bf16[256,5,1792]{2,0,1:T(8,128)(2,1)} async-done(((bf16[64,5,1792]{2,0,1:T(8,128)(2,1)}), bf16[256,5,1792]{2,0,1:T(8,128)(2,1)}) %all-gather.3.cloned.1.call-update) | async-done | bytes 4587536 | tf_op jit(solution)/shard_map/all_gather | solution.py:66
  245.3 8.1 %copy.62 = bf16[256,5,1792]{2,1,0:T(8,128)(2,1)} copy(bf16[256,5,1792]{2,0,1:T(8,128)(2,1)} %all-gather.3.cloned.1.call-done) | data formatting | bytes 9175040 | tf_op jit(solution)/shard_map/all_gather | solution.py:66
  253.3 9.6 %reshape.89 = bf16[1280,1792]{1,0:T(8,128)(2,1)} reshape(bf16[256,5,1792]{2,1,0:T(8,128)(2,1)} %copy.62) | data formatting | bytes 9175040 | tf_op jit(solution)/shard_map/reshape | solution.py:70
  263.0 4.4 fusion.11
  267.5 2.9 fusion.4
  270.4 4.9 fusion.1
  275.4 9.3 %convert_element_type.61 = bf16[4,64,5,1792]{3,2,1,0:T(8,128)(2,1)} reshape(bf16[1280,1792]{1,0:T(8,128)(2,1)} %fusion.1) | data formatting | bytes 9175040 | tf_op jit(solution)/shard_map/convert_element_type | solution.py:91
  284.6 4.7 convolution_convert_fusion.3
  290.6 8.6 %reduce.3 = bf16[64,8960]{1,0:T(8,128)(2,1)} reduce(bf16[64,1,8960]{2,1,0:T(2,128)(2,1)S(1)} %convert_element_type.67, bf16[]{:T(256)} %broadcast.60), dimensions={1}, to_apply=%convert_element_type.67.reduce_sub_computation | reduce | bytes 2293762 | tf_op jit(solution)/shard_map/convert_element_type | solution.py:104
  300.6 117.4 %all_to_all.31 = bf16[64,2,4480]{2,1,0:T(2,128)(2,1)} all-to-all(bf16[64,2,4480]{2,1,0:T(2,128)(2,1)S(1)} %reshape.97), channel_id=1, replica_groups=mesh['ep'=64,'dp'=4] {'ep'}, dimensions={0} | all-to-all | bytes 2293760 | tf_op jit(solution)/shard_map/all_to_all | solution.py:103
  418.0 6.6 %reshape.98 = bf16[64,1,8960]{2,1,0:T(2,128)(2,1)S(1)} reshape(bf16[64,2,4480]{2,1,0:T(2,128)(2,1)} %all_to_all.31) | data formatting | bytes 2293760
  427.0 35.2 %all_to_all.32 = bf16[64,2,4480]{2,1,0:T(2,128)(2,1)} all-to-all(bf16[64,2,4480]{2,1,0:T(2,128)(2,1)S(1)} %reshape.99), channel_id=1, replica_groups=mesh['ep'=64,'dp'=4] {'ep'}, dimensions={0} | all-to-all | bytes 2293760 | tf_op jit(solution)/shard_map/all_to_all | solution.py:30
  462.2 6.3 %all-to-all-start.2 = ((bf16[1,64,5,1792]{3,2,0,1:T(8,128)(2,1)}), bf16[1,64,5,1792]{3,2,0,1:T(8,128)(2,1)}, u32[]{:S(2)}, u32[]{:S(2)}) async-start(bf16[1,64,5,1792]{3,2,0,1:T(8,128)(2,1)} %bitcast.46), calls=%async_computation.3 | async-start | bytes 3670016 | tf_op jit(solution)/shard_map/all_to_all | solution.py:93
  469.5 7.9 %reduce.1 = bf16[64,8960]{1,0:T(8,128)(2,1)} reduce(bf16[64,1,8960]{2,1,0:T(2,128)(2,1)S(1)} %reshape.100, bf16[]{:T(256)} %constant.25), dimensions={1}, to_apply=%all_to_all.23.reduce_sub_computation | reduce | bytes 2293762 | tf_op jit(solution)/shard_map/all_to_all | solution.py:30
  477.4 3.1 reshape.94
  480.5 31.4 %all-to-all-done.2 = bf16[1,64,5,1792]{3,2,0,1:T(8,128)(2,1)} async-done(((bf16[1,64,5,1792]{3,2,0,1:T(8,128)(2,1)}), bf16[1,64,5,1792]{3,2,0,1:T(8,128)(2,1)}, u32[]{:S(2)}, u32[]{:S(2)}) %all-to-all-start.2) | async-done | bytes 1146912 | tf_op jit(solution)/shard_map/all_to_all | solution.py:93
  511.9 2.5 reshape.92
  (56 shorter events, 20.2 us)
Async XLA Ops:
  7.2 188.4 %copy-start = (bf16[1,1792,320]{1,2,0:T(8,128)(2,1)S(1)}, bf16[1,1792,320]{1,2,0:T(8,128)(2,1)}, u32[]{:S(2)}) copy-start(bf16[1,1792,320]{1,2,0:T(8,128)(2,1)} %param.13) | copy-start | bytes 3440644
  7.2 170.6 %all-gather.5.cloned.1.call-start = ((), (), s32[]{:S(2)}) async-start(), calls=%async_computation.7 | async-start | bytes 5734400 | tf_op jit(solution)/shard_map/all_gather | solution.py:65
  71.5 1.3 copy-start.9
  71.5 1.4 copy-start.7
  72.8 172.5 %all-gather.3.cloned.1.call-start = ((), (), s32[]{:S(2)}) async-start(), calls=%async_computation.6 | async-start | bytes 5734400 | tf_op jit(solution)/shard_map/all_gather | solution.py:66
  177.2 285.0 %reduce-scatter.2.cloned.1.call-start = ((), (), s32[]{:S(2)}) async-start(), calls=%async_computation.8 | async-start | bytes 9175040 | tf_op jit(solution)/shard_map/reduce_scatter | solution.py:90
  195.5 4.1 copy-start.3
  195.5 4.2 copy-start.5
  263.0 4.5 copy-start.4
  267.5 2.9 copy-start.6
  418.0 6.6 %copy-start.8 = (s32[64]{0:T(128)S(1)}, s32[64]{0:T(128)}, u32[]{:S(2)}) copy-start(s32[64]{0:T(128)} %param.12) | copy-start | bytes 772
  462.2 6.3 %copy-start.2 = (bf16[64,2,4480]{2,1,0:T(2,128)(2,1)S(1)}, bf16[64,2,4480]{2,1,0:T(2,128)(2,1)}, u32[]{:S(2)}) copy-start(bf16[64,2,4480]{2,1,0:T(2,128)(2,1)} %all_to_all.32) | copy-start | bytes 3440644
  462.2 49.8 %all-to-all-start.2 = ((bf16[1,64,5,1792]{3,2,0,1:T(8,128)(2,1)}), bf16[1,64,5,1792]{3,2,0,1:T(8,128)(2,1)}, u32[]{:S(2)}, u32[]{:S(2)}) async-start(bf16[1,64,5,1792]{3,2,0,1:T(8,128)(2,1)} %bitcast.46), calls=%async_computation.3 | async-start | bytes 3670016 | tf_op jit(solution)/shard_map/all_to_all | solution.py:93
  477.4 38.2 %copy-start.1 = (bf16[1,1792,320]{1,2,0:T(8,128)(2,1)S(1)}, bf16[1,1792,320]{1,2,0:T(8,128)(2,1)}, u32[]{:S(2)}) copy-start(bf16[1,1792,320]{1,2,0:T(8,128)(2,1)} %param.13) | copy-start | bytes 3440644
Sparse Core Ops, SparseCore 0:
  72.9 92.2 all-gather.4
  177.3 67.8 all-gather.2
  284.8 125.5 reduce-scatter.1
where the time goes:
time: 528 us; the launch traced here: 522 us
  blocking collectives  308 us (58%)
  waiting for transfers between devices  74.2 us (14%)
  local copies, waits for them, and re-layouts  69.4 us (13%)
  matrix products  30.2 us (6%)
  other arithmetic  19.6 us (4%)
  between operations  14.3 us (3%)
  starting transfers between devices  6.96 us (1%)
    all_to_all x1, blocking collectives, per_device(): lax.all_to_all(pieces.astype(jnp.bfloat16), 'ep', split_axis=0, concat_ax...  117 us
    all_to_all x1, blocking collectives, per_device(): lax.all_to_all(sent_g, 'ep', split_axis=0, concat_axis=0, tiled=True)  98.8 us
    all_to_all x1, blocking collectives, per_device(): lax.all_to_all(sent_x, 'ep', split_axis=0, concat_axis=0, tiled=True)  56.4 us
    all_gather x1, waiting for transfers between devices, per_device(): lax.all_gather(recv_g, 'dp', axis=0, tiled=True)  42.7 us
    all_to_all x1, blocking collectives, several_exchanges(): lax.all_to_all(section, axis, split_axis=0, concat_axis=0, tiled=True)  35.2 us
    all_to_all x1, waiting for transfers between devices, per_device(): back = lax.all_to_all(summed, 'ep', split_axis=1, concat_axis=1, tiled=True)  31.4 us
  transfers between devices with their start and end apart: 4, of which 2 were waited for; matrix products, arithmetic and copies ran while one was open for 13% of the time, Pallas kernels for 0%

commit v1 on v0

v1 whole, which is shorter than its diff:
```python
import jax
import jax.numpy as jnp
from jax import lax
from jax.experimental import pallas as pl
from jax.experimental.pallas import tpu as pltpu
from jax.sharding import Mesh, PartitionSpec as P

CAP = 5
NZ = 8
PLANE = 16
EXPERTS = 32
INFO = 8
F32 = jnp.float32
BF16 = jnp.bfloat16


def dot(a, b, ca, cb):
    return lax.dot_general(a, b, (((ca,), (cb,)), ((), ())), preferred_element_type=F32)


def expert_sum_kernel(expert_ref, parts_ref, out_ref, total):
    total[...] = jnp.zeros_like(total)

    def add(r, carry):
        e = expert_ref[r]
        total[e] += parts_ref[r].astype(F32)
        return carry

    def put(s, carry):
        out_ref[s] = total[expert_ref[s]].astype(BF16)
        return carry

    lax.fori_loop(0, parts_ref.shape[0], add, 0)
    lax.fori_loop(0, parts_ref.shape[0], put, 0)


def expert_sum(slot_expert, parts):
    return pl.pallas_call(
        expert_sum_kernel,
        out_shape=jax.ShapeDtypeStruct(parts.shape, BF16),
        in_specs=[
            pl.BlockSpec(memory_space=pltpu.SMEM),
            pl.BlockSpec(memory_space=pltpu.VMEM),
        ],
        out_specs=pl.BlockSpec(memory_space=pltpu.VMEM),
        scratch_shapes=[pltpu.VMEM((EXPERTS, *parts.shape[1:]), F32)],
        compiler_params=pltpu.CompilerParams(vmem_limit_bytes=16 * 2**20),
    )(slot_expert, parts)


def per_device(
    tokens, cotangent, slot_choice, gate_values, slot_expert, gate_weight, up_weight, down_weight
):
    rows, width = tokens.shape
    items = 2 * rows
    z_lo = lax.axis_index("zl")
    slot = slot_choice.T.reshape(items)
    weight = gate_values.T.reshape(items)
    order = jnp.arange(items, dtype=jnp.int32)
    earlier = (slot[:, None] == slot[None, :]) & (order[None, :] < order[:, None])
    place = jnp.sum(earlier.astype(jnp.int32), axis=1)
    high = lax.reduce_precision(weight, 8, 7)
    middle = lax.reduce_precision(weight - high, 8, 7)
    low = weight - high - middle
    facts = jnp.stack([slot.astype(F32), place.astype(F32), high, middle, low]).astype(BF16)
    facts = jnp.pad(facts, ((0, INFO - facts.shape[0]), (0, width - items)))
    sent = jnp.concatenate([tokens, facts], axis=0)
    block = rows + INFO

    all_x = lax.all_gather(sent, ("zh", "zl"), axis=0, tiled=True)
    all_g = lax.all_gather(cotangent, ("zh", "zl"), axis=0, tiled=True)

    info = all_x.reshape(NZ, block, width)[:, rows : rows + 5, :items].astype(F32)
    info = info.reshape(NZ, 5, 2, rows)
    source = jnp.arange(NZ, dtype=jnp.int32)[:, None, None]
    code = info[:, 0].astype(jnp.int32) - z_lo * PLANE
    here = (code >= 0) & (code < PLANE)
    code = jnp.where(here, (code * NZ + source) * CAP + info[:, 1].astype(jnp.int32), -1)
    strength = info[:, 2] + info[:, 3] + info[:, 4]
    code = jnp.moveaxis(code, 1, 0)
    strength = jnp.moveaxis(strength, 1, 0)
    held = PLANE * NZ * CAP
    row_ids = jnp.arange(held, dtype=jnp.int32)[:, None]

    code_pad = jnp.pad(code, ((0, 0), (0, 0), (0, INFO)), constant_values=-1).reshape(2, NZ * block)
    pick_x = ((code_pad[0][None, :] == row_ids) | (code_pad[1][None, :] == row_ids)).astype(BF16)
    code = code.reshape(2, NZ * rows)
    strength = strength.reshape(2, NZ * rows)
    first, second = code[0][None, :] == row_ids, code[1][None, :] == row_ids
    pick = (first | second).astype(BF16)
    scale = jnp.sum(
        jnp.where(first, strength[0][None, :], 0.0) + jnp.where(second, strength[1][None, :], 0.0),
        axis=1,
        keepdims=True,
    )
    sent_x = dot(pick_x, all_x, 1, 0).astype(BF16)
    own_x = lax.all_to_all(
        sent_x.reshape(PLANE, NZ * CAP, width), ("y", "x"), split_axis=0, concat_axis=0, tiled=True
    ).reshape(held, width)
    swap = [(0, 1), (1, 0)]
    other_x = lax.ppermute(own_x, "c", swap)
    sent_g = (dot(pick, all_g, 1, 0) * scale).astype(BF16)
    own_g = lax.all_to_all(
        sent_g.reshape(PLANE, NZ * CAP, width), ("y", "x"), split_axis=0, concat_axis=0, tiled=True
    ).reshape(held, width)
    other_g = lax.ppermute(own_g, "c", swap)

    w_gate, w_up, w_down = gate_weight[0], up_weight[0], down_weight[0]

    def half(x, g):
        gate, up = dot(x, w_gate, 1, 0), dot(x, w_up, 1, 0)
        sig = jax.nn.sigmoid(gate)
        act = (gate * sig * up).astype(BF16)
        d_act = dot(g, w_down, 1, 1)
        d_gate = (d_act * up * sig * (1.0 + gate * (1.0 - sig))).astype(BF16)
        d_up = (d_act * gate * sig).astype(BF16)
        return act, d_gate, d_up

    act_o, d_gate_o, d_up_o = half(other_x, other_g)
    for_other = (dot(d_gate_o, w_gate, 1, 1) + dot(d_up_o, w_up, 1, 1)).astype(BF16)
    from_other = lax.ppermute(for_other, "c", swap)
    act, d_gate, d_up = half(own_x, own_g)
    slot_grad = dot(act, own_g, 0, 0) + dot(act_o, other_g, 0, 0)
    own = dot(d_gate, w_gate, 1, 1) + dot(d_up, w_up, 1, 1)
    contribution = (own + from_other.astype(F32)).astype(BF16)

    back = lax.all_to_all(
        contribution.reshape(PLANE, NZ * CAP, width),
        ("y", "x"),
        split_axis=0,
        concat_axis=0,
        tiled=True,
    ).reshape(held, width)
    partial = dot(pick, back, 0, 0).astype(BF16)
    token_grad = lax.psum_scatter(partial, ("zh", "zl"), scatter_dimension=0, tiled=True)

    hidden = slot_grad.shape[0]
    down, across = hidden // 8, width // 128
    n_slots = slot_expert.shape[0]
    each = -(-down * across // n_slots)
    tiles = slot_grad.astype(BF16).reshape(down, 8, across, 128).transpose(0, 2, 1, 3)
    tiles = tiles.reshape(down * across, 8, 128)
    tiles = jnp.pad(tiles, ((0, each * n_slots - down * across), (0, 0), (0, 0)))
    tiles = tiles.reshape(n_slots, each * 8, 128)
    axes = ("zl", "y", "x")
    parts = lax.all_to_all(tiles, axes, split_axis=0, concat_axis=0, tiled=True)
    summed = expert_sum(slot_expert, parts)
    summed = lax.all_to_all(summed, axes, split_axis=0, concat_axis=0, tiled=True)
    summed = summed.reshape(n_slots * each, 8, 128)[: down * across]
    down_grad = summed.reshape(down, across, 8, 128).transpose(0, 2, 1, 3).reshape(1, hidden, width)
    return token_grad, down_grad


def solution(mesh):
    fine = Mesh(mesh.devices.reshape(4, 4, 4, 2, 2), ("zl", "y", "x", "zh", "c"))
    ep, dp = ("zl", "y", "x"), ("zh", "c")
    token = P((*ep, *dp), None)
    return jax.shard_map(
        per_device,
        mesh=fine,
        in_specs=(token, token, token, token, P(), P(ep, None, dp), P(ep, None, dp), P(ep, dp, None)),
        out_specs=(token, P(ep, dp, None)),
        check_vma=False,
    )
```

time: 528 us -> 329 us (0.62)
  blocking collectives: 308 us -> 130 us
  local copies, waits for them, and re-layouts: 69.4 us -> 3.6 us
  waiting for transfers between devices: 74.2 us -> 119 us
  other arithmetic: 19.6 us -> 4.86 us
  matrix products: 30.2 us -> 39.7 us
  starting transfers between devices: 6.96 us -> 15.3 us
    all_to_all x4 -> x3, blocking collectives: 308 us -> 130 us  [the longest x1 50.8 us: per_device(): parts = lax.all_to_all(tiles, axes, split_axis=0, concat_axis=0, tiled=True)]
    all_gather x2, waiting for transfers between devices: 42.7 us -> 89.2 us  [the longest x1 54.4 us: per_device(): all_x = lax.all_gather(sent, ('zh', 'zl'), axis=0, tiled=True)]
    reshape x6 -> x0, local copies, waits for them, and re-layouts: 29.4 us -> none  [the longest x1 9.67 us: per_device(): rows_x = all_x.reshape(-1, width)]
    all_gather x2 -> x0, local copies, waits for them, and re-layouts: 16.1 us -> none  [the longest x1 8.05 us: per_device(): lax.all_gather(recv_x, 'dp', axis=0, tiled=True)]
    convert_element_type x3 -> x1, local copies, waits for them, and re-layouts: 10.5 us -> 0.01 us  [per_device(): place.astype(F32)]
    dot_general x10 -> x15, matrix products: 30.2 us -> 39.7 us  [dot(): lax.dot_general(a, b, (((ca,), (cb,)), ((), ())), preferred_element_type=...]
    unnamed x25 -> x23, local copies, waits for them, and re-layouts: 10.3 us -> 1.48 us
    convert_element_type x2 -> x0, other arithmetic: 8.58 us -> none  [the longest x1 8.57 us: per_device(): pieces.astype(jnp.bfloat16)]
  transfers between devices with their start and end apart: 4 -> 8, of which waited for: 2 -> 3; matrix products, arithmetic and copies ran while one was open for 13% -> 10% of each run, Pallas kernels for 0% -> 1%
where the time goes in v1:
time: 329 us; the launch traced here: 328 us
  blocking collectives  130 us (40%)
  waiting for transfers between devices  119 us (36%)
  matrix products  39.7 us (12%)
  starting transfers between devices  15.3 us (5%)
  between operations  14.1 us (4%)
  other arithmetic  4.86 us (1%)
  local copies, waits for them, and re-layouts  3.6 us (1%)
    all_gather x1, waiting for transfers between devices, per_device(): all_x = lax.all_gather(sent, ('zh', 'zl'), axis=0, tiled=True)  54.4 us
    all_to_all x1, blocking collectives, per_device(): parts = lax.all_to_all(tiles, axes, split_axis=0, concat_axis=0, tiled=True)  50.8 us
    all_to_all x1, blocking collectives, per_device(): lax.all_to_all(summed, axes, split_axis=0, concat_axis=0, tiled=True)  41 us
    dot_general x15, matrix products, dot(): lax.dot_general(a, b, (((ca,), (cb,)), ((), ())), preferred_element_type=...  39.7 us
    all_to_all x1, blocking collectives, per_device(): lax.all_to_all(contribution.reshape(PLANE, NZ * CAP, width), ('y', 'x'),...  37.9 us
    all_gather x1, waiting for transfers between devices, per_device(): all_g = lax.all_gather(cotangent, ('zh', 'zl'), axis=0, tiled=True)  34.8 us
    all_to_all x1, waiting for transfers between devices, per_device(): lax.all_to_all(sent_g.reshape(PLANE, NZ * CAP, width), ('y', 'x'), split_...  29.5 us
    all_to_all x1, starting transfers between devices, per_device(): lax.all_to_all(sent_x.reshape(PLANE, NZ * CAP, width), ('y', 'x'), split_...  7.27 us
  transfers between devices with their start and end apart: 8, of which 3 were waited for; matrix products, arithmetic and copies ran while one was open for 10% of the time, Pallas kernels for 1%

profile of v1, /device:TPU:2, one launch (start us, length us, event | category | flops | bytes accessed | tf_op | source)
XLA Modules:
  0.0 328.4 jit_solution(13772164087807405281)
XLA Ops:
  9.7 1.8 fusion.31
  12.3 54.4 %all-gather.3.cloned.1.call-done = bf16[1088,1792]{1,0:T(8,128)(2,1)} async-done(((bf16[136,1792]{1,0:T(8,128)(2,1)}), bf16[1088,1792]{1,0:T(8,128)(2,1)}) %all-gather.3.cloned.1.call-update) | async-done | bytes 3899408 | tf_op jit(solution)/shard_map/all_gather | solution.py:70
  67.7 6.6 %convolution_convert_fusion.1 = bf16[640,1792]{1,0:T(8,128)(2,1)} fusion(bf16[1088,1792]{1,0:T(8,128)(2,1)} %all-gather.3.cloned.1.call-done, s32[1088]{0:T(1024)S(1)} %eq.91, s32[1088]{0:T(1024)S(1)} %eq.87), kind=kOutput, calls=%fused_computation.4 | convolution fusion | flops 2498846720 | bytes 6201856 | tf_op jit(solution)/shard_map/dot_general | solution.py:18
  74.3 7.3 %all-to-all-start.1 = ((bf16[16,40,1792]{2,1,0:T(8,128)(2,1)}), bf16[16,40,1792]{2,1,0:T(8,128)(2,1)S(1)}, u32[]{:S(2)}, u32[]{:S(2)}) async-start(bf16[16,40,1792]{2,1,0:T(8,128)(2,1)} %bitcast.111), calls=%async_computation.1 | async-start | bytes 4587520 | tf_op jit(solution)/shard_map/all_to_all | solution.py:97
  82.2 34.8 %all-gather.5.cloned.1.call-done = bf16[1024,1792]{1,0:T(8,128)(2,1)} async-done(((bf16[128,1792]{1,0:T(8,128)(2,1)}), bf16[1024,1792]{1,0:T(8,128)(2,1)}) %all-gather.5.cloned.1.call-update) | async-done | bytes 3670032 | tf_op jit(solution)/shard_map/all_gather | solution.py:71
  117.0 6.3 %multiply_convert_fusion = bf16[640,1792]{1,0:T(8,128)(2,1)} fusion(bf16[1024,1792]{1,0:T(8,128)(2,1)} %all-gather.5.cloned.1.call-done, f32[640]{0:T(1024)S(1)} %add_reduce_fusion, s32[1024]{0:T(1024)S(1)} %get-tuple-element.3, s32[1024]{0:T(1024)S(1)} %get-tuple-element.2), kind=kOutput, calls=%fused_computation.2 | convolution fusion | flops 2353070080 | bytes 5974528 | tf_op jit(solution)/shard_map/dot_general | solution.py:18
  123.3 7.3 %all-to-all-start = ((bf16[16,40,1792]{2,1,0:T(8,128)(2,1)}), bf16[16,40,1792]{2,1,0:T(8,128)(2,1)}, u32[]{:S(2)}, u32[]{:S(2)}) async-start(bf16[16,40,1792]{2,1,0:T(8,128)(2,1)} %bitcast.112), calls=%async_computation | async-start | bytes 4587520 | tf_op jit(solution)/shard_map/all_to_all | solution.py:103
  130.7 29.5 %all-to-all-done = bf16[16,40,1792]{2,1,0:T(8,128)(2,1)} async-done(((bf16[16,40,1792]{2,1,0:T(8,128)(2,1)}), bf16[16,40,1792]{2,1,0:T(8,128)(2,1)}, u32[]{:S(2)}, u32[]{:S(2)}) %all-to-all-start) | async-done | bytes 2293792 | tf_op jit(solution)/shard_map/all_to_all | solution.py:103
  160.2 2.8 fusion.14
  163.0 2.8 fusion.21
  165.9 1.4 copy-done.8
  168.4 1.6 fusion.12
  170.0 1.5 add_convert_fusion.1
  172.0 1.1 fusion.18
  173.1 2.7 fusion.28
  176.9 1.6 fusion.16
  178.6 1.5 add_convert_fusion
  180.1 37.9 %all_to_all.25 = bf16[16,40,1792]{2,1,0:T(8,128)(2,1)S(1)} all-to-all(bf16[16,40,1792]{2,1,0:T(8,128)(2,1)S(1)} %bitcast.105), channel_id=1, replica_groups=mesh['zl'=4,'y'=4,'x'=4,'zh'=2,'c'=2] {'y','x'}, dimensions={0} | all-to-all | bytes 4587520 | tf_op jit(solution)/shard_map/all_to_all | solution.py:127
  218.0 4.6 %convolution_convert_fusion = bf16[1024,1792]{1,0:T(8,128)(2,1)} fusion(bf16[640,1792]{1,0:T(8,128)(2,1)S(1)} %bitcast.113, s32[1024]{0:T(1024)S(1)} %get-tuple-element.3, s32[1024]{0:T(1024)S(1)} %get-tuple-element.2), kind=kOutput, calls=%fused_computation.3 | convolution fusion | flops 2352611328 | bytes 5971968 | tf_op jit(solution)/shard_map/dot_general | solution.py:18
  222.7 3.2 fusion.32
  225.9 1.2 fusion.2
  227.2 50.8 %all_to_all.26.parts_ref = bf16[64,72,128]{2,1,0:T(8,128)(2,1)S(1)} all-to-all(bf16[64,72,128]{2,1,0:T(8,128)(2,1)S(1)} %bitcast.106), channel_id=1, replica_groups=mesh['zl'=4,'y'=4,'x'=4,'zh'=2,'c'=2] {'zl','y','x'}, dimensions={0} | all-to-all | bytes 2359296 | tf_op jit(solution)/shard_map/all_to_all | solution.py:146
  278.0 1.7 shard_map.95
  279.7 41.0 %all_to_all.27 = bf16[64,72,128]{2,1,0:T(8,128)(2,1)S(1)} all-to-all(bf16[64,72,128]{2,1,0:T(8,128)(2,1)S(1)} %shard_map.95), channel_id=1, replica_groups=mesh['zl'=4,'y'=4,'x'=4,'zh'=2,'c'=2] {'zl','y','x'}, dimensions={0} | all-to-all | bytes 2359296 | tf_op jit(solution)/shard_map/all_to_all | solution.py:148
  (56 shorter events, 8.8 us)
Async XLA Ops:
  7.2 153.0 %copy-start = (bf16[1,1792,320]{1,2,0:T(8,128)(2,1)S(1)}, bf16[1,1792,320]{1,2,0:T(8,128)(2,1)}, u32[]{:S(2)}) copy-start(bf16[1,1792,320]{1,2,0:T(8,128)(2,1)} %param.13) | copy-start | bytes 3440644
  7.2 59.5 %all-gather.3.cloned.1.call-start = ((), (), s32[]{:S(2)}) async-start(), calls=%async_computation.6 | async-start | bytes 4386816 | tf_op jit(solution)/shard_map/all_gather | solution.py:70
  11.5 105.5 %all-gather.5.cloned.1.call-start = ((), (), s32[]{:S(2)}) async-start(), calls=%async_computation.7 | async-start | bytes 4128768 | tf_op jit(solution)/shard_map/all_gather | solution.py:71
  74.3 49.0 %all-to-all-start.1 = ((bf16[16,40,1792]{2,1,0:T(8,128)(2,1)}), bf16[16,40,1792]{2,1,0:T(8,128)(2,1)S(1)}, u32[]{:S(2)}, u32[]{:S(2)}) async-start(bf16[16,40,1792]{2,1,0:T(8,128)(2,1)} %bitcast.111), calls=%async_computation.1 | async-start | bytes 4587520 | tf_op jit(solution)/shard_map/all_to_all | solution.py:97
  123.3 7.3 %copy-start.3 = (bf16[16,40,1792]{2,1,0:T(8,128)(2,1)}, bf16[16,40,1792]{2,1,0:T(8,128)(2,1)S(1)}, u32[]{:S(2)}) copy-start(bf16[16,40,1792]{2,1,0:T(8,128)(2,1)S(1)} %all-to-all-done.1) | copy-start | bytes 6881284
  123.3 36.9 %all-to-all-start = ((bf16[16,40,1792]{2,1,0:T(8,128)(2,1)}), bf16[16,40,1792]{2,1,0:T(8,128)(2,1)}, u32[]{:S(2)}, u32[]{:S(2)}) async-start(bf16[16,40,1792]{2,1,0:T(8,128)(2,1)} %bitcast.112), calls=%async_computation | async-start | bytes 4587520 | tf_op jit(solution)/shard_map/all_to_all | solution.py:103
  130.5 191.3 %reduce-scatter.2.cloned.1.call-start = ((), (), s32[]{:S(2)}) async-start(), calls=%async_computation.8 | async-start | bytes 4128768 | tf_op jit(solution)/shard_map/reduce_scatter | solution.py:135
  130.6 29.6 %collective-permute-start.1 = (bf16[640,1792]{1,0:T(8,128)(2,1)S(1)}, bf16[640,1792]{1,0:T(8,128)(2,1)}, u32[]{:S(2)}, u32[]{:S(2)}) collective-permute-start(bf16[640,1792]{1,0:T(8,128)(2,1)S(1)} %bitcast.108), channel_id=1, source_target_pairs={{0,1},{1,0},{2,3},{3,2},{4,5},{5,4},{6,7},{7,6},{8,9},{9,8},{10,11... | collective-permute-start | bytes 6881288 | tf_op jit(solution)/shard_map/ppermute | solution.py:101
  160.2 2.9 copy-start.2
  160.2 5.7 %collective-permute-start = (bf16[640,1792]{1,0:T(8,128)(2,1)}, bf16[640,1792]{1,0:T(8,128)(2,1)S(1)}, u32[]{:S(2)}, u32[]{:S(2)}) collective-permute-start(bf16[640,1792]{1,0:T(8,128)(2,1)} %bitcast.21), channel_id=1, source_target_pairs={{0,1},{1,0},{2,3},{3,2},{4,5},{5,4},{6,7},{7,6},{8,9},{9,8},{10,11... | collective-permute-start | bytes 6881288 | tf_op jit(solution)/shard_map/ppermute | solution.py:106
  163.0 4.3 %copy-start.10 = (bf16[1,320,1792]{2,1,0:T(8,128)(2,1)S(1)}, bf16[1,320,1792]{2,1,0:T(8,128)(2,1)}, u32[]{:S(2)}) copy-start(bf16[1,320,1792]{2,1,0:T(8,128)(2,1)} %param.15) | copy-start | bytes 3440644
  165.9 2.5 copy-start.5
  165.9 1.4 copy-start.8
  170.0 2.0 copy-start.4
  171.5 7.1 %collective-permute-start.2 = (bf16[640,1792]{1,0:T(8,128)(2,1)S(1)}, bf16[640,1792]{1,0:T(8,128)(2,1)S(1)}, u32[]{:S(2)}, u32[]{:S(2)}) collective-permute-start(bf16[640,1792]{1,0:T(8,128)(2,1)S(1)} %add_convert_fusion.1), channel_id=1, source_target_pairs={{0,1},{1,0},{2,3},{3,2},{4,5},{5,4},{6,7},{7,6},{8,9},{9,8},{10,11... | collective-permute-start | bytes 6881288 | tf_op jit(solution)/shard_map/ppermute | solution.py:121
  176.9 1.6 copy-start.7
  222.7 3.2 copy-start.6
  222.7 3.2 copy-start.9
  227.1 50.9 %copy-start.1 = (s32[64]{0:T(128)S(1)}, s32[64]{0:T(128)}, u32[]{:S(2)}) copy-start(s32[64]{0:T(128)} %expert_ref.1) | copy-start | bytes 772
Sparse Core Ops, SparseCore 0:
  11.6 54.9 all-gather.2
  68.5 48.4 all-gather.4
  222.8 78.4 reduce-scatter.1

commit v2 on v1

v2 whole, which is shorter than its diff:
```python
import jax
import jax.numpy as jnp
from jax import lax
from jax.experimental import pallas as pl
from jax.experimental.pallas import tpu as pltpu
from jax.sharding import Mesh, PartitionSpec as P

CAP = 5
NZ = 8
PLANE = 16
EXPERTS = 32
F32 = jnp.float32
BF16 = jnp.bfloat16


def dot(a, b, ca, cb):
    return lax.dot_general(a, b, (((ca,), (cb,)), ((), ())), preferred_element_type=F32)


def expert_sum_kernel(expert_ref, parts_ref, out_ref, total):
    count, planes = parts_ref.shape[:2]
    total[...] = jnp.zeros_like(total)

    def add(j, carry):
        for d in range(planes):
            total[expert_ref[d, j]] += parts_ref[j, d].astype(F32)
        return carry

    def put(j, carry):
        for d in range(planes):
            out_ref[j, d] = total[expert_ref[d, j]].astype(BF16)
        return carry

    lax.fori_loop(0, count, add, 0)
    lax.fori_loop(0, count, put, 0)


def expert_sum(expert, parts):
    whole = pl.BlockSpec(memory_space=pltpu.VMEM)
    return pl.pallas_call(
        expert_sum_kernel,
        out_shape=jax.ShapeDtypeStruct(parts.shape, BF16),
        in_specs=[pl.BlockSpec(memory_space=pltpu.SMEM), whole],
        out_specs=whole,
        scratch_shapes=[pltpu.VMEM((EXPERTS, *parts.shape[2:]), F32)],
        compiler_params=pltpu.CompilerParams(vmem_limit_bytes=12 * 2**20),
    )(expert, parts)


def exchange(rows):
    chunks = rows.reshape(PLANE, rows.shape[0] // PLANE, *rows.shape[1:])
    got = lax.all_to_all(chunks, ("y", "x"), split_axis=0, concat_axis=0, tiled=True)
    return got.reshape(rows.shape)


def swapped(rows):
    return lax.ppermute(rows, "c", [(0, 1), (1, 0)])


def after(value, *earlier):
    return lax.optimization_barrier((value, *earlier))[0]


def per_device(
    tokens, cotangent, slot_choice, gate_values, slot_expert, gate_weight, up_weight, down_weight
):
    rows, width = tokens.shape
    items = 2 * rows
    z_lo = lax.axis_index("zl")
    ring = ("zh", "zl")
    all_x = lax.all_gather(tokens, ring, axis=0, tiled=True)
    all_g = lax.all_gather(cotangent, ring, axis=0, tiled=True)

    slot = slot_choice.T.reshape(items)
    order = jnp.arange(items, dtype=jnp.int32)
    earlier = (slot[:, None] == slot[None, :]) & (order[None, :] < order[:, None])
    spot = slot * 8 + jnp.sum(earlier.astype(jnp.int32), axis=1)
    facts = jnp.concatenate([spot.astype(F32).reshape(2, rows), gate_values.T], axis=0)
    info = lax.all_gather(facts, ring, axis=0)
    spot, strength = info[:, :2].astype(jnp.int32), info[:, 2:]
    source = jnp.arange(NZ, dtype=jnp.int32)[:, None, None]
    code = spot // 8 - z_lo * PLANE
    here = (code >= 0) & (code < PLANE)
    code = jnp.where(here, (code * NZ + source) * CAP + spot % 8, -1)
    held = PLANE * NZ * CAP
    code = jnp.moveaxis(code, 1, 0).reshape(2, NZ * rows)
    strength = jnp.moveaxis(strength, 1, 0).reshape(2, NZ * rows)

    row_ids = jnp.arange(held, dtype=jnp.int32)[:, None]
    first, second = code[0][None, :] == row_ids, code[1][None, :] == row_ids
    scale = jnp.sum(
        jnp.where(first, strength[0][None, :], 0.0) + jnp.where(second, strength[1][None, :], 0.0),
        axis=1,
        keepdims=True,
    )
    pick, scale = lax.optimization_barrier(((first | second).astype(BF16), scale))

    w_gate, w_up, w_down = gate_weight[0], up_weight[0], down_weight[0]

    def forward(x):
        gate, up = dot(x, w_gate, 1, 0), dot(x, w_up, 1, 0)
        sig = jax.nn.sigmoid(gate)
        return (gate * sig * up).astype(BF16), up * sig * (1.0 + gate * (1.0 - sig)), gate * sig

    def backward(g, for_gate, for_up):
        d_act = dot(g, w_down, 1, 1)
        return (d_act * for_gate).astype(BF16), (d_act * for_up).astype(BF16)

    x = exchange(dot(pick, all_x, 1, 0).astype(BF16))
    x_o = swapped(x)
    sent_g = (dot(pick, after(all_g, x_o), 1, 0) * scale).astype(BF16)
    x, x_o, sent_g = lax.optimization_barrier((x, x_o, sent_g))
    g = exchange(sent_g)
    forwards = forward(x), forward(x_o)
    forwards, g = lax.optimization_barrier((forwards, g))
    (act, for_gate, for_up), (act_o, for_gate_o, for_up_o) = forwards
    g_o = swapped(g)
    slot_grad = dot(act, g, 0, 0) + dot(act_o, g_o, 0, 0)

    hidden = slot_grad.shape[0]
    down, across = hidden // 8, width // 128
    n_slots = slot_expert.shape[0]
    planes = n_slots // PLANE
    each = -(-down * across // n_slots)
    tiles = slot_grad.astype(BF16).reshape(down, 8, across, 128).transpose(0, 2, 1, 3)
    tiles = tiles.reshape(down * across, 8, 128)
    tiles = jnp.pad(tiles, ((0, each * n_slots - down * across), (0, 0), (0, 0)))
    tiles = tiles.reshape(planes, PLANE, each * 8, 128)

    def of_plane(v, d, dim):
        return lax.dynamic_index_in_dim(v, z_lo ^ d, dim, False)

    def along_z(piece, d):
        return lax.ppermute(piece, "zl", [(z, z ^ d) for z in range(planes)]) if d else piece

    sent = lax.optimization_barrier((g, g_o, *[of_plane(tiles, d, 0) for d in range(planes)]))
    g, g_o = sent[:2]
    pieces = [along_z(piece, d) for d, piece in enumerate(sent[2:])]

    d_gate_o, d_up_o = backward(g_o, for_gate_o, for_up_o)
    for_other = (dot(d_gate_o, w_gate, 1, 1) + dot(d_up_o, w_up, 1, 1)).astype(BF16)
    from_other = swapped(for_other)
    d_gate, d_up = backward(g, for_gate, for_up)
    own = dot(d_gate, w_gate, 1, 1) + dot(d_up, w_up, 1, 1)
    back = exchange((own + from_other.astype(F32)).astype(BF16))
    parts = jnp.stack(pieces, axis=1)
    back, parts = lax.optimization_barrier((back, parts))
    parts = exchange(parts)
    partial = dot(pick, back, 0, 0).astype(BF16)
    token_grad = lax.psum_scatter(partial, ring, scatter_dimension=0, tiled=True)

    expert = slot_expert.reshape(planes, PLANE)
    expert = jnp.stack([of_plane(expert, d, 0) for d in range(planes)])
    sums = exchange(expert_sum(expert, parts))
    summed = jnp.stack([along_z(sums[:, d], d) for d in range(planes)])
    summed = jnp.concatenate([of_plane(summed, z, 0) for z in range(planes)])
    summed = summed.reshape(n_slots * each, 8, 128)[: down * across]
    down_grad = summed.reshape(down, across, 8, 128).transpose(0, 2, 1, 3).reshape(1, hidden, width)
    return token_grad, down_grad


def solution(mesh):
    fine = Mesh(mesh.devices.reshape(4, 4, 4, 2, 2), ("zl", "y", "x", "zh", "c"))
    ep, dp = ("zl", "y", "x"), ("zh", "c")
    token = P((*ep, *dp), None)
    return jax.shard_map(
        per_device,
        mesh=fine,
        in_specs=(token, token, token, token, P(), P(ep, None, dp), P(ep, None, dp), P(ep, dp, None)),
        out_specs=(token, P(ep, dp, None)),
        check_vma=False,
    )
```

time: 329 us -> 309 us (0.939)
  blocking collectives: 130 us -> 82.9 us
  starting transfers between devices: 15.3 us -> 33.1 us
  matrix products: 39.7 us -> 45.7 us
    all_to_all x3 -> x2, blocking collectives: 130 us -> 57.5 us  [exchange(): lax.all_to_all(chunks, ('y', 'x'), split_axis=0, concat_axis=0, tiled=True)]
    all_gather x2, waiting for transfers between devices: 89.2 us -> 34.3 us  [the longest x1 24.8 us: per_device(): all_x = lax.all_gather(tokens, ring, axis=0, tiled=True)]
    ppermute x3 -> x9, waiting for transfers between devices: 0.01 us -> 47.7 us  [the longest x6 43.5 us: along_z(): lax.ppermute(piece, 'zl', [(z, z ^ d) for z in range(planes)])]
    all_gather x0 -> x1, blocking collectives: none -> 25.4 us  [per_device(): info = lax.all_gather(facts, ring, axis=0)]
    all_to_all x2 -> x3, starting transfers between devices: 14.5 us -> 24.7 us  [exchange(): lax.all_to_all(chunks, ('y', 'x'), split_axis=0, concat_axis=0, tiled=True)]
    all_to_all x2 -> x3, waiting for transfers between devices: 29.5 us -> 38.5 us  [exchange(): lax.all_to_all(chunks, ('y', 'x'), split_axis=0, concat_axis=0, tiled=True)]
    ppermute x3 -> x9, starting transfers between devices: 0.6 us -> 8.35 us  [the longest x6 8.12 us: along_z(): lax.ppermute(piece, 'zl', [(z, z ^ d) for z in range(planes)])]
    dot_general x15, matrix products: 39.7 us -> 45.7 us  [dot(): lax.dot_general(a, b, (((ca,), (cb,)), ((), ())), preferred_element_type=...]
  transfers between devices with their start and end apart: 8 -> 15, of which waited for: 3 -> 12; matrix products, arithmetic and copies ran while one was open for 10% -> 10% of each run, Pallas kernels for 1% -> 0%
where the time goes in v2:
time: 309 us; the launch traced here: 308 us
  waiting for transfers between devices  122 us (39%)
  blocking collectives  82.9 us (27%)
  matrix products  45.7 us (15%)
  starting transfers between devices  33.1 us (11%)
  between operations  14.1 us (5%)
  other arithmetic  6.28 us (2%)
  local copies, waits for them, and re-layouts  3.16 us (1%)
    all_to_all x2, blocking collectives, exchange(): lax.all_to_all(chunks, ('y', 'x'), split_axis=0, concat_axis=0, tiled=True)  57.5 us
    dot_general x15, matrix products, dot(): lax.dot_general(a, b, (((ca,), (cb,)), ((), ())), preferred_element_type=...  45.7 us
    ppermute x6, waiting for transfers between devices, along_z(): lax.ppermute(piece, 'zl', [(z, z ^ d) for z in range(planes)])  43.5 us
    all_to_all x3, waiting for transfers between devices, exchange(): lax.all_to_all(chunks, ('y', 'x'), split_axis=0, concat_axis=0, tiled=True)  38.5 us
    all_gather x1, blocking collectives, per_device(): info = lax.all_gather(facts, ring, axis=0)  25.4 us
    all_gather x1, waiting for transfers between devices, per_device(): all_x = lax.all_gather(tokens, ring, axis=0, tiled=True)  24.8 us
    all_to_all x3, starting transfers between devices, exchange(): lax.all_to_all(chunks, ('y', 'x'), split_axis=0, concat_axis=0, tiled=True)  24.7 us
    all_gather x1, waiting for transfers between devices, per_device(): all_g = lax.all_gather(cotangent, ring, axis=0, tiled=True)  9.44 us
  transfers between devices with their start and end apart: 15, of which 12 were waited for; matrix products, arithmetic and copies ran while one was open for 10% of the time, Pallas kernels for 0%

profile of v2, /device:TPU:2, one launch (start us, length us, event | category | flops | bytes accessed | tf_op | source)
XLA Modules:
  0.0 308.4 jit_solution(15387813462838722470)
XLA Ops:
  11.0 25.4 %all-gather.1 = f32[8,4,128]{2,1,0:T(4,128)S(1)} all-gather(f32[1,4,128]{2,1,0:T(4,128)S(1)} %maximum_bitcast_fusion), channel_id=2, replica_groups=mesh['zl'=4,'y'=4,'x'=4,'zh'=2,'c'=2] {'zh','zl'}, dimensions={0}, use_global_device_ids=true | all-gather | bytes 18432 | tf_op jit(solution)/shard_map/all_gather | solution.py:79
  38.0 24.8 %all-gather.5.cloned.1.call-done = bf16[1024,1792]{1,0:T(8,128)(2,1)} async-done(((bf16[128,1792]{1,0:T(8,128)(2,1)}), bf16[1024,1792]{1,0:T(8,128)(2,1)}) %all-gather.5.cloned.1.call-update) | async-done | bytes 3670032 | tf_op jit(solution)/shard_map/all_gather | solution.py:71
  62.8 4.6 %convolution_convert_fusion.1 = bf16[640,1792]{1,0:T(8,128)(2,1)S(1)} fusion(bf16[640,1024]{1,0:T(8,128)(2,1)S(1)} %fusion.2, bf16[1024,1792]{1,0:T(8,128)(2,1)} %all-gather.5.cloned.1.call-done), kind=kOutput, calls=%fused_computation.4 | convolution fusion | flops 2349957120 | bytes 7274496 | tf_op jit(solution)/shard_map/dot_general | solution.py:17
  67.4 36.2 %all_to_all.25 = bf16[16,40,1792]{2,1,0:T(8,128)(2,1)S(1)} all-to-all(bf16[16,40,1792]{2,1,0:T(8,128)(2,1)S(1)} %bitcast.138), channel_id=1, replica_groups=mesh['zl'=4,'y'=4,'x'=4,'zh'=2,'c'=2] {'y','x'}, dimensions={0} | all-to-all | bytes 4587520 | tf_op jit(solution)/shard_map/all_to_all | solution.py:52
  103.6 9.4 %all-gather.7.cloned.1.call-done = bf16[1024,1792]{1,0:T(8,128)(2,1)} async-done(((bf16[128,1792]{1,0:T(8,128)(2,1)}), bf16[1024,1792]{1,0:T(8,128)(2,1)}) %all-gather.7.cloned.1.call-update) | async-done | bytes 3670032 | tf_op jit(solution)/shard_map/all_gather | solution.py:72
  113.1 6.4 %multiply_convert_fusion = bf16[640,1792]{1,0:T(8,128)(2,1)} fusion(bf16[640,1024]{1,0:T(8,128)(2,1)} %copy-done.7, bf16[1024,1792]{1,0:T(8,128)(2,1)} %all-gather.7.cloned.1.call-done, f32[640]{0:T(1024)S(1)} %reduce), kind=kOutput, calls=%fused_computation.2 | convolution fusion | flops 2351104000 | bytes 7277056 | tf_op jit(solution)/shard_map/dot_general | solution.py:17
  119.5 7.3 %all-to-all-start.1 = ((bf16[16,40,1792]{2,1,0:T(8,128)(2,1)}), bf16[16,40,1792]{2,1,0:T(8,128)(2,1)S(1)}, u32[]{:S(2)}, u32[]{:S(2)}) async-start(bf16[16,40,1792]{2,1,0:T(8,128)(2,1)} %bitcast.137), calls=%async_computation.1 | async-start | bytes 4587520 | tf_op jit(solution)/shard_map/all_to_all | solution.py:52
  126.7 3.1 %fusion.11 = f32[640,320]{0,1:T(8,128)S(1)} fusion(bf16[640,1792]{1,0:T(8,128)(2,1)} %bitcast.135, bf16[1,1792,320]{1,2,0:T(8,128)(2,1)} %param.14), kind=kOutput, calls=%fused_computation.23 | convolution fusion | flops 734003200 | bytes 4259840 | tf_op jit(solution)/shard_map/dot_general | solution.py:17
  129.9 2.9 fusion.9
  135.4 4.1 %add_multiply_fusion = (f32[640,320]{0,1:T(8,128)}, bf16[640,320]{0,1:T(8,128)(2,1)}, f32[640,320]{0,1:T(8,128)}) fusion(f32[640,320]{0,1:T(8,128)S(1)} %fusion.9, bf16[640,1792]{1,0:T(8,128)(2,1)} %collective-permute-done, bf16[1,1792,320]{1,2,0:T(8,128)(2,1)S(1)} %copy-done), kind=kOutput, calls=%fused_computation.37 | convolution fusion | flops 736256000 | bytes 6307840 | tf_op jit(solution)/shard_map/dot_general | solution.py:17
  139.6 16.7 %all-to-all-done.1 = bf16[16,40,1792]{2,1,0:T(8,128)(2,1)S(1)} async-done(((bf16[16,40,1792]{2,1,0:T(8,128)(2,1)}), bf16[16,40,1792]{2,1,0:T(8,128)(2,1)S(1)}, u32[]{:S(2)}, u32[]{:S(2)}) %all-to-all-start.1) | async-done | bytes 2293792 | tf_op jit(solution)/shard_map/all_to_all | solution.py:52
  178.4 8.7 %all-to-all-start.2 = ((bf16[16,40,1792]{2,1,0:T(8,128)(2,1)}), bf16[16,40,1792]{2,1,0:T(8,128)(2,1)S(1)}, u32[]{:S(2)}, u32[]{:S(2)}) async-start(bf16[16,40,1792]{2,1,0:T(8,128)(2,1)} %bitcast.27), calls=%async_computation.2 | async-start | bytes 4587520 | tf_op jit(solution)/shard_map/all_to_all | solution.py:52
  187.3 3.5 %collective-permute-start.4 = (bf16[16,72,128]{2,1,0:T(8,128)(2,1)}, bf16[16,72,128]{2,1,0:T(8,128)(2,1)S(1)}, u32[]{:S(2)}, u32[]{:S(2)}) collective-permute-start(bf16[16,72,128]{2,1,0:T(8,128)(2,1)} %get-tuple-element.40), channel_id=1, source_target_pairs={{0,128},{64,192},{128,0},{192,64},{1,129},{65,193},{129,1},{193,65... | collective-permute-start | bytes 884744 | tf_op jit(solution)/shard_map/ppermute | solution.py:134
  191.7 10.1 %collective-permute-done.3 = bf16[16,72,128]{2,1,0:T(8,128)(2,1)S(1)} collective-permute-done((bf16[16,72,128]{2,1,0:T(8,128)(2,1)}, bf16[16,72,128]{2,1,0:T(8,128)(2,1)S(1)}, u32[]{:S(2)}, u32[]{:S(2)}) %collective-permute-start.3) | collective-permute-done | bytes 294944 | tf_op jit(solution)/shard_map/ppermute | solution.py:134
  201.7 9.8 %collective-permute-done.4 = bf16[16,72,128]{2,1,0:T(8,128)(2,1)S(1)} collective-permute-done((bf16[16,72,128]{2,1,0:T(8,128)(2,1)}, bf16[16,72,128]{2,1,0:T(8,128)(2,1)S(1)}, u32[]{:S(2)}, u32[]{:S(2)}) %collective-permute-start.4) | collective-permute-done | bytes 294944 | tf_op jit(solution)/shard_map/ppermute | solution.py:134
  213.6 5.2 %all-to-all-done.2 = bf16[16,40,1792]{2,1,0:T(8,128)(2,1)S(1)} async-done(((bf16[16,40,1792]{2,1,0:T(8,128)(2,1)}), bf16[16,40,1792]{2,1,0:T(8,128)(2,1)S(1)}, u32[]{:S(2)}, u32[]{:S(2)}) %all-to-all-start.2) | async-done | bytes 2293792 | tf_op jit(solution)/shard_map/all_to_all | solution.py:52
  218.8 6.2 %convolution_convert_fusion = bf16[1024,1792]{1,0:T(8,128)(2,1)} fusion(bf16[640,1024]{1,0:T(8,128)(2,1)} %copy-done.7, bf16[640,1792]{1,0:T(8,128)(2,1)S(1)} %bitcast.133), kind=kOutput, calls=%fused_computation.3 | convolution fusion | flops 2350645248 | bytes 7274496 | tf_op jit(solution)/shard_map/dot_general | solution.py:17
  225.0 8.7 %all-to-all-start.3 = ((bf16[16,1,4,72,128]{4,3,2,1,0:T(8,128)(2,1)}), bf16[16,1,4,72,128]{4,3,2,1,0:T(8,128)(2,1)S(1)}, u32[]{:S(2)}, u32[]{:S(2)}) async-start(bf16[16,1,4,72,128]{4,3,2,1,0:T(8,128)(2,1)} %bitcast.33), calls=%async_computation.4 | async-start | bytes 2359296 | tf_op jit(solution)/shard_map/all_to_all | solution.py:52
  233.9 16.6 %all-to-all-done.3 = bf16[16,1,4,72,128]{4,3,2,1,0:T(8,128)(2,1)S(1)} async-done(((bf16[16,1,4,72,128]{4,3,2,1,0:T(8,128)(2,1)}), bf16[16,1,4,72,128]{4,3,2,1,0:T(8,128)(2,1)S(1)}, u32[]{:S(2)}, u32[]{:S(2)}) %all-to-all-start.3) | async-done | bytes 1179680 | tf_op jit(solution)/shard_map/all_to_all | solution.py:52
  251.8 21.2 %all_to_all.26 = bf16[16,1,4,72,128]{4,3,2,1,0:T(8,128)(2,1)S(1)} all-to-all(bf16[16,1,4,72,128]{4,3,2,1,0:T(8,128)(2,1)S(1)} %bitcast.126), channel_id=1, replica_groups=mesh['zl'=4,'y'=4,'x'=4,'zh'=2,'c'=2] {'y','x'}, dimensions={0} | all-to-all | bytes 2359296 | tf_op jit(solution)/shard_map/all_to_all | solution.py:52
  273.2 3.1 %collective-permute-start.8 = (bf16[16,72,128]{2,1,0:T(8,128)(2,1)S(1)}, bf16[16,72,128]{2,1,0:T(8,128)(2,1)S(1)}, u32[]{:S(2)}, u32[]{:S(2)}) collective-permute-start(bf16[16,72,128]{2,1,0:T(8,128)(2,1)S(1)} %get-tuple-element.54), channel_id=1, source_target_pairs={{0,192},{64,128},{128,64},{192,0},{1,193},{65,129},{129,65},{193,1... | collective-permute-start | bytes 884744 | tf_op jit(solution)/shard_map/ppermute | solution.py:134
  276.7 7.2 %collective-permute-done.6 = bf16[16,72,128]{2,1,0:T(8,128)(2,1)S(1)} collective-permute-done((bf16[16,72,128]{2,1,0:T(8,128)(2,1)S(1)}, bf16[16,72,128]{2,1,0:T(8,128)(2,1)S(1)}, u32[]{:S(2)}, u32[]{:S(2)}) %collective-permute-start.6) | collective-permute-done | bytes 294944 | tf_op jit(solution)/shard_map/ppermute | solution.py:134
  284.0 6.5 %collective-permute-done.8 = bf16[16,72,128]{2,1,0:T(8,128)(2,1)S(1)} collective-permute-done((bf16[16,72,128]{2,1,0:T(8,128)(2,1)S(1)}, bf16[16,72,128]{2,1,0:T(8,128)(2,1)S(1)}, u32[]{:S(2)}, u32[]{:S(2)}) %collective-permute-start.8) | collective-permute-done | bytes 294944 | tf_op jit(solution)/shard_map/ppermute | solution.py:134
  290.5 9.9 %collective-permute-done.7 = bf16[16,72,128]{2,1,0:T(8,128)(2,1)S(1)} collective-permute-done((bf16[16,72,128]{2,1,0:T(8,128)(2,1)S(1)}, bf16[16,72,128]{2,1,0:T(8,128)(2,1)S(1)}, u32[]{:S(2)}, u32[]{:S(2)}) %collective-permute-start.7) | collective-permute-done | bytes 294944 | tf_op jit(solution)/shard_map/ppermute | solution.py:134
  (76 shorter events, 36.6 us)
Async XLA Ops:
  7.2 125.6 %copy-start = (bf16[1,1792,320]{1,2,0:T(8,128)(2,1)S(1)}, bf16[1,1792,320]{1,2,0:T(8,128)(2,1)}, u32[]{:S(2)}) copy-start(bf16[1,1792,320]{1,2,0:T(8,128)(2,1)} %param.13) | copy-start | bytes 3440644
  7.2 55.6 %all-gather.5.cloned.1.call-start = ((), (), s32[]{:S(2)}) async-start(), calls=%async_computation.6 | async-start | bytes 4128768 | tf_op jit(solution)/shard_map/all_gather | solution.py:71
  7.9 105.2 %all-gather.7.cloned.1.call-start = ((), (), s32[]{:S(2)}) async-start(), calls=%async_computation.7 | async-start | bytes 4128768 | tf_op jit(solution)/shard_map/all_gather | solution.py:72
  38.0 29.4 %copy-start.7 = (bf16[640,1024]{1,0:T(8,128)(2,1)}, bf16[640,1024]{1,0:T(8,128)(2,1)S(1)}, u32[]{:S(2)}) copy-start(bf16[640,1024]{1,0:T(8,128)(2,1)S(1)} %fusion.2) | copy-start | bytes 3932164
  103.6 15.8 %copy-start.3 = (bf16[16,40,1792]{2,1,0:T(8,128)(2,1)}, bf16[16,40,1792]{2,1,0:T(8,128)(2,1)S(1)}, u32[]{:S(2)}) copy-start(bf16[16,40,1792]{2,1,0:T(8,128)(2,1)S(1)} %all_to_all.25) | copy-start | bytes 6881284
  103.6 9.5 %collective-permute-start = (bf16[640,1792]{1,0:T(8,128)(2,1)S(1)}, bf16[640,1792]{1,0:T(8,128)(2,1)}, u32[]{:S(2)}, u32[]{:S(2)}) collective-permute-start(bf16[640,1792]{1,0:T(8,128)(2,1)S(1)} %bitcast.134), channel_id=1, source_target_pairs={{0,1},{1,0},{2,3},{3,2},{4,5},{5,4},{6,7},{7,6},{8,9},{9,8},{10,11... | collective-permute-start | bytes 6881288 | tf_op jit(solution)/shard_map/ppermute | solution.py:57
  119.5 36.8 %all-to-all-start.1 = ((bf16[16,40,1792]{2,1,0:T(8,128)(2,1)}), bf16[16,40,1792]{2,1,0:T(8,128)(2,1)S(1)}, u32[]{:S(2)}, u32[]{:S(2)}) async-start(bf16[16,40,1792]{2,1,0:T(8,128)(2,1)} %bitcast.137), calls=%async_computation.1 | async-start | bytes 4587520 | tf_op jit(solution)/shard_map/all_to_all | solution.py:52
  126.7 3.1 %copy-start.1 = (bf16[1,1792,320]{1,2,0:T(8,128)(2,1)S(1)}, bf16[1,1792,320]{1,2,0:T(8,128)(2,1)}, u32[]{:S(2)}) copy-start(bf16[1,1792,320]{1,2,0:T(8,128)(2,1)} %param.14) | copy-start | bytes 3440644
  129.9 2.9 copy-start.4
  156.3 4.6 %collective-permute-start.1 = (bf16[640,1792]{1,0:T(8,128)(2,1)S(1)}, bf16[640,1792]{1,0:T(8,128)(2,1)}, u32[]{:S(2)}, u32[]{:S(2)}) collective-permute-start(bf16[640,1792]{1,0:T(8,128)(2,1)S(1)} %bitcast.127), channel_id=1, source_target_pairs={{0,1},{1,0},{2,3},{3,2},{4,5},{5,4},{6,7},{7,6},{8,9},{9,8},{10,11... | collective-permute-start | bytes 6881288 | tf_op jit(solution)/shard_map/ppermute | solution.py:57
  156.3 4.6 %copy-start.12 = (bf16[640,320]{0,1:T(8,128)(2,1)S(1)}, bf16[640,320]{0,1:T(8,128)(2,1)}, u32[]{:S(2)}) copy-start(bf16[640,320]{0,1:T(8,128)(2,1)} %get-tuple-element.31) | copy-start | bytes 1228804
  165.3 2.8 copy-start.6
  171.0 4.5 %collective-permute-start.2 = (bf16[640,1792]{1,0:T(8,128)(2,1)S(1)}, bf16[640,1792]{1,0:T(8,128)(2,1)S(1)}, u32[]{:S(2)}, u32[]{:S(2)}) collective-permute-start(bf16[640,1792]{1,0:T(8,128)(2,1)S(1)} %add_convert_fusion.1), channel_id=1, source_target_pairs={{0,1},{1,0},{2,3},{3,2},{4,5},{5,4},{6,7},{7,6},{8,9},{9,8},{10,11... | collective-permute-start | bytes 6881288 | tf_op jit(solution)/shard_map/ppermute | solution.py:57
  172.4 3.2 %copy-start.8 = (f32[640,320]{0,1:T(8,128)S(1)}, f32[640,320]{0,1:T(8,128)}, u32[]{:S(2)}) copy-start(f32[640,320]{0,1:T(8,128)} %get-tuple-element.34) | copy-start | bytes 2457604
  178.4 40.4 %all-to-all-start.2 = ((bf16[16,40,1792]{2,1,0:T(8,128)(2,1)}), bf16[16,40,1792]{2,1,0:T(8,128)(2,1)S(1)}, u32[]{:S(2)}, u32[]{:S(2)}) async-start(bf16[16,40,1792]{2,1,0:T(8,128)(2,1)} %bitcast.27), calls=%async_computation.2 | async-start | bytes 4587520 | tf_op jit(solution)/shard_map/all_to_all | solution.py:52
  187.1 114.7 %reduce-scatter.2.cloned.1.call-start = ((), (), s32[]{:S(2)}) async-start(), calls=%async_computation.8 | async-start | bytes 4128768 | tf_op jit(solution)/shard_map/reduce_scatter | solution.py:150
  187.2 14.6 %collective-permute-start.3 = (bf16[16,72,128]{2,1,0:T(8,128)(2,1)}, bf16[16,72,128]{2,1,0:T(8,128)(2,1)S(1)}, u32[]{:S(2)}, u32[]{:S(2)}) collective-permute-start(bf16[16,72,128]{2,1,0:T(8,128)(2,1)} %get-tuple-element.39), channel_id=1, source_target_pairs={{0,64},{64,0},{128,192},{192,128},{1,65},{65,1},{129,193},{193,129... | collective-permute-start | bytes 884744 | tf_op jit(solution)/shard_map/ppermute | solution.py:134
  187.3 24.2 %collective-permute-start.4 = (bf16[16,72,128]{2,1,0:T(8,128)(2,1)}, bf16[16,72,128]{2,1,0:T(8,128)(2,1)S(1)}, u32[]{:S(2)}, u32[]{:S(2)}) collective-permute-start(bf16[16,72,128]{2,1,0:T(8,128)(2,1)} %get-tuple-element.40), channel_id=1, source_target_pairs={{0,128},{64,192},{128,0},{192,64},{1,129},{65,193},{129,1},{193,65... | collective-permute-start | bytes 884744 | tf_op jit(solution)/shard_map/ppermute | solution.py:134
  190.8 20.7 %collective-permute-start.5 = (bf16[16,72,128]{2,1,0:T(8,128)(2,1)}, bf16[16,72,128]{2,1,0:T(8,128)(2,1)S(1)}, u32[]{:S(2)}, u32[]{:S(2)}) collective-permute-start(bf16[16,72,128]{2,1,0:T(8,128)(2,1)} %get-tuple-element.41), channel_id=1, source_target_pairs={{0,192},{64,128},{128,64},{192,0},{1,193},{65,129},{129,65},{193,1... | collective-permute-start | bytes 884744 | tf_op jit(solution)/shard_map/ppermute | solution.py:134
  225.0 8.7 %copy-start.10 = (s32[64]{0:T(128)S(1)}, s32[64]{0:T(128)}, u32[]{:S(2)}) copy-start(s32[64]{0:T(128)} %param.12) | copy-start | bytes 772
  225.0 25.5 %all-to-all-start.3 = ((bf16[16,1,4,72,128]{4,3,2,1,0:T(8,128)(2,1)}), bf16[16,1,4,72,128]{4,3,2,1,0:T(8,128)(2,1)S(1)}, u32[]{:S(2)}, u32[]{:S(2)}) async-start(bf16[16,1,4,72,128]{4,3,2,1,0:T(8,128)(2,1)} %bitcast.33), calls=%async_computation.4 | async-start | bytes 2359296 | tf_op jit(solution)/shard_map/all_to_all | solution.py:52
  273.1 10.9 %collective-permute-start.6 = (bf16[16,72,128]{2,1,0:T(8,128)(2,1)S(1)}, bf16[16,72,128]{2,1,0:T(8,128)(2,1)S(1)}, u32[]{:S(2)}, u32[]{:S(2)}) collective-permute-start(bf16[16,72,128]{2,1,0:T(8,128)(2,1)S(1)} %get-tuple-element.53), channel_id=1, source_target_pairs={{0,64},{64,0},{128,192},{192,128},{1,65},{65,1},{129,193},{193,129... | collective-permute-start | bytes 884744 | tf_op jit(solution)/shard_map/ppermute | solution.py:134
  273.2 17.3 %collective-permute-start.8 = (bf16[16,72,128]{2,1,0:T(8,128)(2,1)S(1)}, bf16[16,72,128]{2,1,0:T(8,128)(2,1)S(1)}, u32[]{:S(2)}, u32[]{:S(2)}) collective-permute-start(bf16[16,72,128]{2,1,0:T(8,128)(2,1)S(1)} %get-tuple-element.54), channel_id=1, source_target_pairs={{0,192},{64,128},{128,64},{192,0},{1,193},{65,129},{129,65},{193,1... | collective-permute-start | bytes 884744 | tf_op jit(solution)/shard_map/ppermute | solution.py:134
  276.3 24.1 %collective-permute-start.7 = (bf16[16,72,128]{2,1,0:T(8,128)(2,1)S(1)}, bf16[16,72,128]{2,1,0:T(8,128)(2,1)S(1)}, u32[]{:S(2)}, u32[]{:S(2)}) collective-permute-start(bf16[16,72,128]{2,1,0:T(8,128)(2,1)S(1)} %get-tuple-element.55), channel_id=1, source_target_pairs={{0,128},{64,192},{128,0},{192,64},{1,129},{65,193},{129,1},{193,65... | collective-permute-start | bytes 884744 | tf_op jit(solution)/shard_map/ppermute | solution.py:134
  (4 other events, 5.9 us)
Sparse Core Ops, SparseCore 0:
  9.8 52.9 all-gather.4
  64.6 48.4 all-gather.6
  225.2 50.4 reduce-scatter.1

commit v3 on v2

--- a/solution.py
+++ b/solution.py
@@ -6,6 +6,7 @@
 from jax.sharding import Mesh, PartitionSpec as P
 
 CAP = 5
+INFO = 8
 NZ = 8
 PLANE = 16
 EXPERTS = 32
@@ -61,39 +62,70 @@
     return lax.optimization_barrier((value, *earlier))[0]
 
 
+def ring_steps(own):
+    def at(z):
+        return (z % NZ) % 4 * 2 + (z % NZ) // 4
+
+    up = [(at(z), at(z + 1)) for z in range(NZ)]
+    down = [(at(z), at(z - 1)) for z in range(NZ)]
+    below, above = [own], [own]
+    for step in range(NZ // 2):
+        below.append(lax.ppermute(below[-1], ("zl", "zh"), up))
+        if step < NZ // 2 - 1:
+            above.append(lax.ppermute(above[-1], ("zl", "zh"), down))
+    return above + below[:0:-1], (below[3], above[3])
+
+
 def per_device(
     tokens, cotangent, slot_choice, gate_values, slot_expert, gate_weight, up_weight, down_weight
 ):
     rows, width = tokens.shape
     items = 2 * rows
-    z_lo = lax.axis_index("zl")
+    z_lo, z_hi = lax.axis_index("zl"), lax.axis_index("zh")
+    turn = z_hi * 4 + z_lo
     ring = ("zh", "zl")
-    all_x = lax.all_gather(tokens, ring, axis=0, tiled=True)
-    all_g = lax.all_gather(cotangent, ring, axis=0, tiled=True)
-
     slot = slot_choice.T.reshape(items)
+    weight = gate_values.T.reshape(items)
     order = jnp.arange(items, dtype=jnp.int32)
     earlier = (slot[:, None] == slot[None, :]) & (order[None, :] < order[:, None])
-    spot = slot * 8 + jnp.sum(earlier.astype(jnp.int32), axis=1)
-    facts = jnp.concatenate([spot.astype(F32).reshape(2, rows), gate_values.T], axis=0)
-    info = lax.all_gather(facts, ring, axis=0)
-    spot, strength = info[:, :2].astype(jnp.int32), info[:, 2:]
-    source = jnp.arange(NZ, dtype=jnp.int32)[:, None, None]
-    code = spot // 8 - z_lo * PLANE
+    place = jnp.sum(earlier.astype(jnp.int32), axis=1)
+    high = lax.reduce_precision(weight, 8, 7)
+    middle = lax.reduce_precision(weight - high, 8, 7)
+    low = weight - high - middle
+    facts = jnp.stack([slot.astype(F32), place.astype(F32), high, middle, low]).astype(BF16)
+    facts = jnp.pad(facts, ((0, INFO - facts.shape[0]), (0, width - items)))
+    block = rows + INFO
+
+    x_pieces, started = ring_steps(jnp.concatenate([tokens, facts], axis=0))
+    all_g = lax.all_gather(after(cotangent, *started), ring, axis=0, tiled=True)
+
+    info = jnp.stack([p[rows : rows + 5, :items] for p in x_pieces]).astype(F32).reshape(NZ, 5, 2, rows)
+    source = ((jnp.arange(NZ, dtype=jnp.int32) + turn) % NZ)[:, None, None]
+    code = info[:, 0].astype(jnp.int32) - z_lo * PLANE
     here = (code >= 0) & (code < PLANE)
-    code = jnp.where(here, (code * NZ + source) * CAP + spot % 8, -1)
+    code = jnp.where(here, (code * NZ + source) * CAP + info[:, 1].astype(jnp.int32), -1)
+    strength = info[:, 2] + info[:, 3] + info[:, 4]
     held = PLANE * NZ * CAP
-    code = jnp.moveaxis(code, 1, 0).reshape(2, NZ * rows)
-    strength = jnp.moveaxis(strength, 1, 0).reshape(2, NZ * rows)
-
     row_ids = jnp.arange(held, dtype=jnp.int32)[:, None]
+
+    def flat(v):
+        return jnp.moveaxis(v, 1, 0).reshape(2, -1)
+
+    def from_zero(v):
+        return flat(lax.dynamic_slice_in_dim(jnp.concatenate([v, v], axis=0), NZ - turn, NZ, axis=0))
+
+    code_x = flat(jnp.pad(code, ((0, 0), (0, 0), (0, INFO)), constant_values=-1))
+    pick_x = ((code_x[0][None, :] == row_ids) | (code_x[1][None, :] == row_ids)).astype(BF16)
+    pick_x, *x_pieces = lax.optimization_barrier((pick_x, *x_pieces))
+    all_x = jnp.concatenate(x_pieces, axis=0)
+    code, strength = from_zero(code), from_zero(strength)
     first, second = code[0][None, :] == row_ids, code[1][None, :] == row_ids
     scale = jnp.sum(
         jnp.where(first, strength[0][None, :], 0.0) + jnp.where(second, strength[1][None, :], 0.0),
         axis=1,
         keepdims=True,
     )
-    pick, scale = lax.optimization_barrier(((first | second).astype(BF16), scale))
+    pick = (first | second).astype(BF16)
 
     w_gate, w_up, w_down = gate_weight[0], up_weight[0], down_weight[0]
 
@@ -106,17 +138,25 @@
         d_act = dot(g, w_down, 1, 1)
         return (d_act * for_gate).astype(BF16), (d_act * for_up).astype(BF16)
 
-    x = exchange(dot(pick, all_x, 1, 0).astype(BF16))
+    x = exchange(dot(pick_x, all_x, 1, 0).astype(BF16))
+    sent_g = (dot(pick, all_g, 1, 0) * scale).astype(BF16)
+    x, sent_g = lax.optimization_barrier((x, sent_g))
     x_o = swapped(x)
-    sent_g = (dot(pick, after(all_g, x_o), 1, 0) * scale).astype(BF16)
-    x, x_o, sent_g = lax.optimization_barrier((x, x_o, sent_g))
     g = exchange(sent_g)
     forwards = forward(x), forward(x_o)
     forwards, g = lax.optimization_barrier((forwards, g))
     (act, for_gate, for_up), (act_o, for_gate_o, for_up_o) = forwards
     g_o = swapped(g)
+    d_gate, d_up = backward(g, for_gate, for_up)
+    own = dot(d_gate, w_gate, 1, 1) + dot(d_up, w_up, 1, 1)
+    d_gate_o, d_up_o = backward(g_o, for_gate_o, for_up_o)
+    for_other = (dot(d_gate_o, w_gate, 1, 1) + dot(d_up_o, w_up, 1, 1)).astype(BF16)
+    from_other = swapped(for_other)
+    contribution = (own + from_other.astype(F32)).astype(BF16)
+    contribution, act, act_o, g, g_o = lax.optimization_barrier((contribution, act, act_o, g, g_o))
+    back = exchange(contribution)
+
     slot_grad = dot(act, g, 0, 0) + dot(act_o, g_o, 0, 0)
-
     hidden = slot_grad.shape[0]
     down, across = hidden // 8, width // 128
     n_slots = slot_expert.shape[0]
@@ -133,16 +173,8 @@
     def along_z(piece, d):
         return lax.ppermute(piece, "zl", [(z, z ^ d) for z in range(planes)]) if d else piece
 
-    sent = lax.optimization_barrier((g, g_o, *[of_plane(tiles, d, 0) for d in range(planes)]))
-    g, g_o = sent[:2]
-    pieces = [along_z(piece, d) for d, piece in enumerate(sent[2:])]
-
-    d_gate_o, d_up_o = backward(g_o, for_gate_o, for_up_o)
-    for_other = (dot(d_gate_o, w_gate, 1, 1) + dot(d_up_o, w_up, 1, 1)).astype(BF16)
-    from_other = swapped(for_other)
-    d_gate, d_up = backward(g, for_gate, for_up)
-    own = dot(d_gate, w_gate, 1, 1) + dot(d_up, w_up, 1, 1)
-    back = exchange((own + from_other.astype(F32)).astype(BF16))
+    sent = [of_plane(tiles, d, 0) for d in range(planes)]
+    pieces = [along_z(piece, d) for d, piece in enumerate(sent)]
     parts = jnp.stack(pieces, axis=1)
     back, parts = lax.optimization_barrier((back, parts))
     parts = exchange(parts)

time: 309 us -> 300 us (0.971)
  blocking collectives: 82.9 us -> 21.3 us
  waiting for transfers between devices: 122 us -> 144 us
  starting transfers between devices: 33.1 us -> 53.1 us
  local copies, waits for them, and re-layouts: 3.16 us -> 9.46 us
    ppermute x0 -> x7, waiting for transfers between devices: none -> 39 us  [the longest x3 27.8 us: ring_steps(): above.append(lax.ppermute(above[-1], ('zl', 'zh'), down))]
    all_to_all x2 -> x1, blocking collectives: 57.5 us -> 21.3 us  [exchange(): lax.all_to_all(chunks, ('y', 'x'), split_axis=0, concat_axis=0, tiled=True)]
    all_gather x1 -> x0, blocking collectives: 25.4 us -> none  [per_device(): info = lax.all_gather(facts, ring, axis=0)]
    all_gather x2 -> x1, waiting for transfers between devices: 34.3 us -> 18.6 us  [per_device(): all_g = lax.all_gather(after(cotangent, *started), ring, axis=0, tiled=True)]
    ppermute x0 -> x7, starting transfers between devices: none -> 13.3 us  [the longest x3 13.3 us: ring_steps(): above.append(lax.ppermute(above[-1], ('zl', 'zh'), down))]
    all_to_all x3 -> x4, starting transfers between devices: 24.7 us -> 30.3 us  [exchange(): lax.all_to_all(chunks, ('y', 'x'), split_axis=0, concat_axis=0, tiled=True)]
    unnamed x26 -> x40, local copies, waits for them, and re-layouts: 0.66 us -> 4.73 us
    all_to_all x3 -> x4, waiting for transfers between devices: 38.5 us -> 37.2 us  [exchange(): lax.all_to_all(chunks, ('y', 'x'), split_axis=0, concat_axis=0, tiled=True)]
  transfers between devices with their start and end apart: 15 -> 22, of which waited for: 12 -> 15; matrix products, arithmetic and copies ran while one was open for 10% -> 15% of each run, Pallas kernels for 0% -> 0%
where the time goes in v3:
time: 300 us; the launch traced here: 299 us
  waiting for transfers between devices  144 us (48%)
  starting transfers between devices  53.1 us (18%)
  matrix products  46.7 us (16%)
  blocking collectives  21.3 us (7%)
  between operations  14.5 us (5%)
  local copies, waits for them, and re-layouts  9.46 us (3%)
  other arithmetic  8.75 us (3%)
    dot_general x15, matrix products, dot(): lax.dot_general(a, b, (((ca,), (cb,)), ((), ())), preferred_element_type=...  46.7 us
    ppermute x6, waiting for transfers between devices, along_z(): lax.ppermute(piece, 'zl', [(z, z ^ d) for z in range(planes)])  44.2 us
    all_to_all x4, waiting for transfers between devices, exchange(): lax.all_to_all(chunks, ('y', 'x'), split_axis=0, concat_axis=0, tiled=True)  37.2 us
    all_to_all x4, starting transfers between devices, exchange(): lax.all_to_all(chunks, ('y', 'x'), split_axis=0, concat_axis=0, tiled=True)  30.3 us
    ppermute x3, waiting for transfers between devices, ring_steps(): above.append(lax.ppermute(above[-1], ('zl', 'zh'), down))  27.8 us
    all_to_all x1, blocking collectives, exchange(): lax.all_to_all(chunks, ('y', 'x'), split_axis=0, concat_axis=0, tiled=True)  21.3 us
    all_gather x1, waiting for transfers between devices, per_device(): all_g = lax.all_gather(after(cotangent, *started), ring, axis=0, tiled=True)  18.6 us
    ppermute x3, starting transfers between devices, ring_steps(): above.append(lax.ppermute(above[-1], ('zl', 'zh'), down))  13.3 us
  transfers between devices with their start and end apart: 22, of which 15 were waited for; matrix products, arithmetic and copies ran while one was open for 15% of the time, Pallas kernels for 0%

profile of v3, /device:TPU:2, one launch (start us, length us, event | category | flops | bytes accessed | tf_op | source)
XLA Modules:
  0.0 298.8 jit_solution(8521163631586613555)
XLA Ops:
  10.7 5.9 %collective-permute-start = (bf16[136,1792]{1,0:T(8,128)(2,1)S(1)}, bf16[136,1792]{1,0:T(8,128)(2,1)S(1)}, u32[]{:S(2)}, u32[]{:S(2)}) collective-permute-start(bf16[136,1792]{1,0:T(8,128)(2,1)S(1)} %fusion.31), channel_id=1, source_target_pairs={{0,194},{64,0},{128,64},{192,128},{2,192},{66,2},{130,66},{194,130... | collective-permute-start | bytes 1462280 | tf_op jit(solution)/shard_map/ppermute | solution.py:75
  16.7 10.4 %collective-permute-done = bf16[136,1792]{1,0:T(8,128)(2,1)S(1)} collective-permute-done((bf16[136,1792]{1,0:T(8,128)(2,1)S(1)}, bf16[136,1792]{1,0:T(8,128)(2,1)S(1)}, u32[]{:S(2)}, u32[]{:S(2)}) %collective-permute-start) | collective-permute-done | bytes 487456 | tf_op jit(solution)/shard_map/ppermute | solution.py:75
  27.1 3.7 %collective-permute-start.1 = (bf16[136,1792]{1,0:T(8,128)(2,1)S(1)}, bf16[136,1792]{1,0:T(8,128)(2,1)S(1)}, u32[]{:S(2)}, u32[]{:S(2)}) collective-permute-start(bf16[136,1792]{1,0:T(8,128)(2,1)S(1)} %collective-permute-done), channel_id=1, source_target_pairs={{0,194},{64,0},{128,64},{192,128},{2,192},{66,2},{130,66},{194,130... | collective-permute-start | bytes 1462280 | tf_op jit(solution)/shard_map/ppermute | solution.py:75
  30.8 9.5 %collective-permute-done.1 = bf16[136,1792]{1,0:T(8,128)(2,1)S(1)} collective-permute-done((bf16[136,1792]{1,0:T(8,128)(2,1)S(1)}, bf16[136,1792]{1,0:T(8,128)(2,1)S(1)}, u32[]{:S(2)}, u32[]{:S(2)}) %collective-permute-start.1) | collective-permute-done | bytes 487456 | tf_op jit(solution)/shard_map/ppermute | solution.py:75
  44.7 7.9 %collective-permute-done.2 = bf16[136,1792]{1,0:T(8,128)(2,1)S(1)} collective-permute-done((bf16[136,1792]{1,0:T(8,128)(2,1)S(1)}, bf16[136,1792]{1,0:T(8,128)(2,1)S(1)}, u32[]{:S(2)}, u32[]{:S(2)}) %collective-permute-start.2) | collective-permute-done | bytes 487456 | tf_op jit(solution)/shard_map/ppermute | solution.py:75
  59.7 8.5 %collective-permute-done.6 = bf16[136,1792]{1,0:T(8,128)(2,1)} collective-permute-done((bf16[136,1792]{1,0:T(8,128)(2,1)}, bf16[136,1792]{1,0:T(8,128)(2,1)}, u32[]{:S(2)}, u32[]{:S(2)}) %collective-permute-start.6) | collective-permute-done | bytes 487456 | tf_op jit(solution)/shard_map/ppermute | solution.py:73
  72.7 4.3 %convolution_convert_fusion.1 = bf16[640,1792]{1,0:T(8,128)(2,1)} fusion(bf16[640,1088]{1,0:T(8,128)(2,1)S(1)} %fusion.1, bf16[1088,1792]{1,0:T(8,128)(2,1)S(1)} %constant_dynamic-update-slice_fusion.12), kind=kOutput, calls=%fused_computation.4 | convolution fusion | flops 2496757760 | bytes 7585792 | tf_op jit(solution)/shard_map/dot_general | solution.py:18
  77.1 7.5 %all-to-all-start = ((bf16[16,40,1792]{2,1,0:T(8,128)(2,1)}), bf16[16,40,1792]{2,1,0:T(8,128)(2,1)}, u32[]{:S(2)}, u32[]{:S(2)}) async-start(bf16[16,40,1792]{2,1,0:T(8,128)(2,1)} %bitcast.18), calls=%async_computation | async-start | bytes 4587520 | tf_op jit(solution)/shard_map/all_to_all | solution.py:53
  85.3 18.6 %all-gather.2.cloned.1.call-done = bf16[1024,1792]{1,0:T(8,128)(2,1)} async-done(((bf16[128,1792]{1,0:T(8,128)(2,1)}), bf16[1024,1792]{1,0:T(8,128)(2,1)}) %all-gather.2.cloned.1.call-update) | async-done | bytes 3670032 | tf_op jit(solution)/shard_map/all_gather | solution.py:100
  104.0 6.2 %multiply_convert_fusion = bf16[640,1792]{1,0:T(8,128)(2,1)} fusion(bf16[1024,1792]{1,0:T(8,128)(2,1)} %all-gather.2.cloned.1.call-done, f32[640]{0:T(1024)S(1)} %add_reduce_fusion, s32[1024]{0:T(1024)S(1)} %bitcast.198, s32[1024]{0:T(1024)S(1)} %bitcast.195), kind=kOutput, calls=%fused_computation.2 | convolution fusion | flops 2353070080 | bytes 5974528 | tf_op jit(solution)/shard_map/dot_general | solution.py:18
  111.4 6.9 %all-to-all-start.1 = ((bf16[16,40,1792]{2,1,0:T(8,128)(2,1)}), bf16[16,40,1792]{2,1,0:T(8,128)(2,1)}, u32[]{:S(2)}, u32[]{:S(2)}) async-start(bf16[16,40,1792]{2,1,0:T(8,128)(2,1)} %bitcast.185), calls=%async_computation.1 | async-start | bytes 4587520 | tf_op jit(solution)/shard_map/all_to_all | solution.py:53
  121.1 3.9 %add_multiply_fusion.1 = (f32[640,320]{0,1:T(8,128)S(1)}, bf16[640,320]{0,1:T(8,128)(2,1)}, f32[640,320]{0,1:T(8,128)}) fusion(f32[640,320]{0,1:T(8,128)S(1)} %fusion.18, bf16[640,1792]{1,0:T(8,128)(2,1)} %bitcast.19, bf16[1,1792,320]{1,2,0:T(8,128)(2,1)S(1)} %copy-done), kind=kOutput, calls=%fused_computation.50 | convolution fusion | flops 736256000 | bytes 6307840 | tf_op jit(solution)/shard_map/dot_general | solution.py:18
  127.7 4.2 %add_multiply_fusion = (f32[640,320]{0,1:T(8,128)}, bf16[640,320]{0,1:T(8,128)(2,1)}, f32[640,320]{0,1:T(8,128)}) fusion(f32[640,320]{0,1:T(8,128)S(1)} %fusion.16, bf16[640,1792]{1,0:T(8,128)(2,1)} %collective-permute-done.7, bf16[1,1792,320]{1,2,0:T(8,128)(2,1)S(1)} %copy-done), kind=kOutput, calls=%fused_computation.46 | convolution fusion | flops 736256000 | bytes 6307840 | tf_op jit(solution)/shard_map/dot_general | solution.py:18
  131.9 19.4 %all-to-all-done.1 = bf16[16,40,1792]{2,1,0:T(8,128)(2,1)} async-done(((bf16[16,40,1792]{2,1,0:T(8,128)(2,1)}), bf16[16,40,1792]{2,1,0:T(8,128)(2,1)}, u32[]{:S(2)}, u32[]{:S(2)}) %all-to-all-start.1) | async-done | bytes 2293792 | tf_op jit(solution)/shard_map/all_to_all | solution.py:53
  151.2 4.6 %collective-permute-done.8 = bf16[640,1792]{1,0:T(8,128)(2,1)S(1)} collective-permute-done((bf16[640,1792]{1,0:T(8,128)(2,1)}, bf16[640,1792]{1,0:T(8,128)(2,1)S(1)}, u32[]{:S(2)}, u32[]{:S(2)}) %collective-permute-start.8) | collective-permute-done | bytes 2293792 | tf_op jit(solution)/shard_map/ppermute | solution.py:58
  170.4 8.5 %all-to-all-start.2 = ((bf16[16,40,1792]{2,1,0:T(8,128)(2,1)}), bf16[16,40,1792]{2,1,0:T(8,128)(2,1)S(1)}, u32[]{:S(2)}, u32[]{:S(2)}) async-start(bf16[16,40,1792]{2,1,0:T(8,128)(2,1)} %bitcast.29), calls=%async_computation.2 | async-start | bytes 4587520 | tf_op jit(solution)/shard_map/all_to_all | solution.py:53
  189.4 7.4 %collective-permute-done.12 = bf16[16,72,128]{2,1,0:T(8,128)(2,1)S(1)} collective-permute-done((bf16[16,72,128]{2,1,0:T(8,128)(2,1)S(1)}, bf16[16,72,128]{2,1,0:T(8,128)(2,1)S(1)}, u32[]{:S(2)}, u32[]{:S(2)}) %collective-permute-start.12) | collective-permute-done | bytes 294944 | tf_op jit(solution)/shard_map/ppermute | solution.py:174
  196.7 14.8 %collective-permute-done.11 = bf16[16,72,128]{2,1,0:T(8,128)(2,1)S(1)} collective-permute-done((bf16[16,72,128]{2,1,0:T(8,128)(2,1)S(1)}, bf16[16,72,128]{2,1,0:T(8,128)(2,1)S(1)}, u32[]{:S(2)}, u32[]{:S(2)}) %collective-permute-start.11) | collective-permute-done | bytes 294944 | tf_op jit(solution)/shard_map/ppermute | solution.py:174
  212.7 4.5 %convolution_convert_fusion = bf16[1024,1792]{1,0:T(8,128)(2,1)} fusion(bf16[640,1792]{1,0:T(8,128)(2,1)S(1)} %bitcast.184, s32[1024]{0:T(1024)S(1)} %bitcast.199, s32[1024]{0:T(1024)S(1)} %bitcast.196), kind=kOutput, calls=%fused_computation.3 | convolution fusion | flops 2352611328 | bytes 5971968 | tf_op jit(solution)/shard_map/dot_general | solution.py:18
  217.3 7.3 %all-to-all-start.3 = ((bf16[16,1,4,72,128]{4,3,2,1,0:T(8,128)(2,1)}), bf16[16,1,4,72,128]{4,3,2,1,0:T(8,128)(2,1)S(1)}, u32[]{:S(2)}, u32[]{:S(2)}) async-start(bf16[16,1,4,72,128]{4,3,2,1,0:T(8,128)(2,1)} %bitcast.42), calls=%async_computation.4 | async-start | bytes 2359296 | tf_op jit(solution)/shard_map/all_to_all | solution.py:53
  224.7 16.6 %all-to-all-done.3 = bf16[16,1,4,72,128]{4,3,2,1,0:T(8,128)(2,1)S(1)} async-done(((bf16[16,1,4,72,128]{4,3,2,1,0:T(8,128)(2,1)}), bf16[16,1,4,72,128]{4,3,2,1,0:T(8,128)(2,1)S(1)}, u32[]{:S(2)}, u32[]{:S(2)}) %all-to-all-start.3) | async-done | bytes 1179680 | tf_op jit(solution)/shard_map/all_to_all | solution.py:53
  242.6 21.3 %all_to_all.25 = bf16[16,1,4,72,128]{4,3,2,1,0:T(8,128)(2,1)S(1)} all-to-all(bf16[16,1,4,72,128]{4,3,2,1,0:T(8,128)(2,1)S(1)} %bitcast.180), channel_id=1, replica_groups=mesh['zl'=4,'y'=4,'x'=4,'zh'=2,'c'=2] {'y','x'}, dimensions={0} | all-to-all | bytes 2359296 | tf_op jit(solution)/shard_map/all_to_all | solution.py:53
  268.4 7.4 %collective-permute-done.15 = bf16[16,72,128]{2,1,0:T(8,128)(2,1)S(1)} collective-permute-done((bf16[16,72,128]{2,1,0:T(8,128)(2,1)S(1)}, bf16[16,72,128]{2,1,0:T(8,128)(2,1)S(1)}, u32[]{:S(2)}, u32[]{:S(2)}) %collective-permute-start.15) | collective-permute-done | bytes 294944 | tf_op jit(solution)/shard_map/ppermute | solution.py:174
  275.8 14.6 %collective-permute-done.14 = bf16[16,72,128]{2,1,0:T(8,128)(2,1)S(1)} collective-permute-done((bf16[16,72,128]{2,1,0:T(8,128)(2,1)S(1)}, bf16[16,72,128]{2,1,0:T(8,128)(2,1)S(1)}, u32[]{:S(2)}, u32[]{:S(2)}) %collective-permute-start.14) | collective-permute-done | bytes 294944 | tf_op jit(solution)/shard_map/ppermute | solution.py:174
  (130 shorter events, 60.2 us)
Async XLA Ops:
  7.2 113.9 %copy-start = (bf16[1,1792,320]{1,2,0:T(8,128)(2,1)S(1)}, bf16[1,1792,320]{1,2,0:T(8,128)(2,1)}, u32[]{:S(2)}) copy-start(bf16[1,1792,320]{1,2,0:T(8,128)(2,1)} %param.13) | copy-start | bytes 3440644
  7.2 96.8 %all-gather.2.cloned.1.call-start = ((), (), s32[]{:S(2)}) async-start(), calls=%async_computation.6 | async-start | bytes 4128768 | tf_op jit(solution)/shard_map/all_gather | solution.py:100
  10.7 16.3 %collective-permute-start = (bf16[136,1792]{1,0:T(8,128)(2,1)S(1)}, bf16[136,1792]{1,0:T(8,128)(2,1)S(1)}, u32[]{:S(2)}, u32[]{:S(2)}) collective-permute-start(bf16[136,1792]{1,0:T(8,128)(2,1)S(1)} %fusion.31), channel_id=1, source_target_pairs={{0,194},{64,0},{128,64},{192,128},{2,192},{66,2},{130,66},{194,130... | collective-permute-start | bytes 1462280 | tf_op jit(solution)/shard_map/ppermute | solution.py:75
  16.7 14.1 %collective-permute-start.3 = (bf16[136,1792]{1,0:T(8,128)(2,1)S(1)}, bf16[136,1792]{1,0:T(8,128)(2,1)S(1)}, u32[]{:S(2)}, u32[]{:S(2)}) collective-permute-start(bf16[136,1792]{1,0:T(8,128)(2,1)S(1)} %fusion.31), channel_id=1, source_target_pairs={{0,64},{64,128},{128,192},{192,2},{2,66},{66,130},{130,194},{194,0... | collective-permute-start | bytes 1462280 | tf_op jit(solution)/shard_map/ppermute | solution.py:73
  27.1 13.2 %collective-permute-start.1 = (bf16[136,1792]{1,0:T(8,128)(2,1)S(1)}, bf16[136,1792]{1,0:T(8,128)(2,1)S(1)}, u32[]{:S(2)}, u32[]{:S(2)}) collective-permute-start(bf16[136,1792]{1,0:T(8,128)(2,1)S(1)} %collective-permute-done), channel_id=1, source_target_pairs={{0,194},{64,0},{128,64},{192,128},{2,192},{66,2},{130,66},{194,130... | collective-permute-start | bytes 1462280 | tf_op jit(solution)/shard_map/ppermute | solution.py:75
  30.8 13.2 %collective-permute-start.4 = (bf16[136,1792]{1,0:T(8,128)(2,1)S(1)}, bf16[136,1792]{1,0:T(8,128)(2,1)S(1)}, u32[]{:S(2)}, u32[]{:S(2)}) collective-permute-start(bf16[136,1792]{1,0:T(8,128)(2,1)S(1)} %collective-permute-done.3), channel_id=1, source_target_pairs={{0,64},{64,128},{128,192},{192,2},{2,66},{66,130},{130,194},{194,0... | collective-permute-start | bytes 1462280 | tf_op jit(solution)/shard_map/ppermute | solution.py:73
  40.3 12.3 %collective-permute-start.2 = (bf16[136,1792]{1,0:T(8,128)(2,1)S(1)}, bf16[136,1792]{1,0:T(8,128)(2,1)S(1)}, u32[]{:S(2)}, u32[]{:S(2)}) collective-permute-start(bf16[136,1792]{1,0:T(8,128)(2,1)S(1)} %collective-permute-done.1), channel_id=1, source_target_pairs={{0,194},{64,0},{128,64},{192,128},{2,192},{66,2},{130,66},{194,130... | collective-permute-start | bytes 1462280 | tf_op jit(solution)/shard_map/ppermute | solution.py:75
  44.0 12.1 %collective-permute-start.5 = (bf16[136,1792]{1,0:T(8,128)(2,1)S(1)}, bf16[136,1792]{1,0:T(8,128)(2,1)}, u32[]{:S(2)}, u32[]{:S(2)}) collective-permute-start(bf16[136,1792]{1,0:T(8,128)(2,1)S(1)} %collective-permute-done.4), channel_id=1, source_target_pairs={{0,64},{64,128},{128,192},{192,2},{2,66},{66,130},{130,194},{194,0... | collective-permute-start | bytes 1462280 | tf_op jit(solution)/shard_map/ppermute | solution.py:73
  56.8 11.4 %collective-permute-start.6 = (bf16[136,1792]{1,0:T(8,128)(2,1)}, bf16[136,1792]{1,0:T(8,128)(2,1)}, u32[]{:S(2)}, u32[]{:S(2)}) collective-permute-start(bf16[136,1792]{1,0:T(8,128)(2,1)} %collective-permute-done.5), channel_id=1, source_target_pairs={{0,64},{64,128},{128,192},{192,2},{2,66},{66,130},{130,194},{194,0... | collective-permute-start | bytes 1462280 | tf_op jit(solution)/shard_map/ppermute | solution.py:73
  77.1 34.3 %all-to-all-start = ((bf16[16,40,1792]{2,1,0:T(8,128)(2,1)}), bf16[16,40,1792]{2,1,0:T(8,128)(2,1)}, u32[]{:S(2)}, u32[]{:S(2)}) async-start(bf16[16,40,1792]{2,1,0:T(8,128)(2,1)} %bitcast.18), calls=%async_computation | async-start | bytes 4587520 | tf_op jit(solution)/shard_map/all_to_all | solution.py:53
  111.4 13.6 %collective-permute-start.7 = (bf16[640,1792]{1,0:T(8,128)(2,1)}, bf16[640,1792]{1,0:T(8,128)(2,1)}, u32[]{:S(2)}, u32[]{:S(2)}) collective-permute-start(bf16[640,1792]{1,0:T(8,128)(2,1)} %bitcast.19), channel_id=1, source_target_pairs={{0,1},{1,0},{2,3},{3,2},{4,5},{5,4},{6,7},{7,6},{8,9},{9,8},{10,11... | collective-permute-start | bytes 6881288 | tf_op jit(solution)/shard_map/ppermute | solution.py:58
  111.4 39.8 %all-to-all-start.1 = ((bf16[16,40,1792]{2,1,0:T(8,128)(2,1)}), bf16[16,40,1792]{2,1,0:T(8,128)(2,1)}, u32[]{:S(2)}, u32[]{:S(2)}) async-start(bf16[16,40,1792]{2,1,0:T(8,128)(2,1)} %bitcast.185), calls=%async_computation.1 | async-start | bytes 4587520 | tf_op jit(solution)/shard_map/all_to_all | solution.py:53
  151.2 8.4 %copy-start.3 = (f32[640,320]{0,1:T(8,128)S(1)}, f32[640,320]{0,1:T(8,128)}, u32[]{:S(2)}) copy-start(f32[640,320]{0,1:T(8,128)} %get-tuple-element.43) | copy-start | bytes 2457604
  151.2 4.7 %collective-permute-start.8 = (bf16[640,1792]{1,0:T(8,128)(2,1)}, bf16[640,1792]{1,0:T(8,128)(2,1)S(1)}, u32[]{:S(2)}, u32[]{:S(2)}) collective-permute-start(bf16[640,1792]{1,0:T(8,128)(2,1)} %bitcast.27), channel_id=1, source_target_pairs={{0,1},{1,0},{2,3},{3,2},{4,5},{5,4},{6,7},{7,6},{8,9},{9,8},{10,11... | collective-permute-start | bytes 6881288 | tf_op jit(solution)/shard_map/ppermute | solution.py:58
  162.6 4.7 %collective-permute-start.9 = (bf16[640,1792]{1,0:T(8,128)(2,1)S(1)}, bf16[640,1792]{1,0:T(8,128)(2,1)S(1)}, u32[]{:S(2)}, u32[]{:S(2)}) collective-permute-start(bf16[640,1792]{1,0:T(8,128)(2,1)S(1)} %add_convert_fusion.1), channel_id=1, source_target_pairs={{0,1},{1,0},{2,3},{3,2},{4,5},{5,4},{6,7},{7,6},{8,9},{9,8},{10,11... | collective-permute-start | bytes 6881288 | tf_op jit(solution)/shard_map/ppermute | solution.py:58
  170.4 42.3 %all-to-all-start.2 = ((bf16[16,40,1792]{2,1,0:T(8,128)(2,1)}), bf16[16,40,1792]{2,1,0:T(8,128)(2,1)S(1)}, u32[]{:S(2)}, u32[]{:S(2)}) async-start(bf16[16,40,1792]{2,1,0:T(8,128)(2,1)} %bitcast.29), calls=%async_computation.2 | async-start | bytes 4587520 | tf_op jit(solution)/shard_map/all_to_all | solution.py:53
  179.0 113.0 %reduce-scatter.2.cloned.1.call-start = ((), (), s32[]{:S(2)}) async-start(), calls=%async_computation.7 | async-start | bytes 4128768 | tf_op jit(solution)/shard_map/reduce_scatter | solution.py:182
  184.9 11.9 %collective-permute-start.12 = (bf16[16,72,128]{2,1,0:T(8,128)(2,1)S(1)}, bf16[16,72,128]{2,1,0:T(8,128)(2,1)S(1)}, u32[]{:S(2)}, u32[]{:S(2)}) collective-permute-start(bf16[16,72,128]{2,1,0:T(8,128)(2,1)S(1)} %get-tuple-element.73), channel_id=1, source_target_pairs={{0,192},{64,128},{128,64},{192,0},{1,193},{65,129},{129,65},{193,1... | collective-permute-start | bytes 884744 | tf_op jit(solution)/shard_map/ppermute | solution.py:174
  186.7 24.8 %collective-permute-start.11 = (bf16[16,72,128]{2,1,0:T(8,128)(2,1)S(1)}, bf16[16,72,128]{2,1,0:T(8,128)(2,1)S(1)}, u32[]{:S(2)}, u32[]{:S(2)}) collective-permute-start(bf16[16,72,128]{2,1,0:T(8,128)(2,1)S(1)} %get-tuple-element.74), channel_id=1, source_target_pairs={{0,128},{64,192},{128,0},{192,64},{1,129},{65,193},{129,1},{193,65... | collective-permute-start | bytes 884744 | tf_op jit(solution)/shard_map/ppermute | solution.py:174
  186.7 24.8 %collective-permute-start.10 = (bf16[16,72,128]{2,1,0:T(8,128)(2,1)S(1)}, bf16[16,72,128]{2,1,0:T(8,128)(2,1)S(1)}, u32[]{:S(2)}, u32[]{:S(2)}) collective-permute-start(bf16[16,72,128]{2,1,0:T(8,128)(2,1)S(1)} %get-tuple-element.75), channel_id=1, source_target_pairs={{0,64},{64,0},{128,192},{192,128},{1,65},{65,1},{129,193},{193,129... | collective-permute-start | bytes 884744 | tf_op jit(solution)/shard_map/ppermute | solution.py:174
  217.3 24.0 %all-to-all-start.3 = ((bf16[16,1,4,72,128]{4,3,2,1,0:T(8,128)(2,1)}), bf16[16,1,4,72,128]{4,3,2,1,0:T(8,128)(2,1)S(1)}, u32[]{:S(2)}, u32[]{:S(2)}) async-start(bf16[16,1,4,72,128]{4,3,2,1,0:T(8,128)(2,1)} %bitcast.42), calls=%async_computation.4 | async-start | bytes 2359296 | tf_op jit(solution)/shard_map/all_to_all | solution.py:53
  263.9 11.9 %collective-permute-start.15 = (bf16[16,72,128]{2,1,0:T(8,128)(2,1)S(1)}, bf16[16,72,128]{2,1,0:T(8,128)(2,1)S(1)}, u32[]{:S(2)}, u32[]{:S(2)}) collective-permute-start(bf16[16,72,128]{2,1,0:T(8,128)(2,1)S(1)} %get-tuple-element.70), channel_id=1, source_target_pairs={{0,192},{64,128},{128,64},{192,0},{1,193},{65,129},{129,65},{193,1... | collective-permute-start | bytes 884744 | tf_op jit(solution)/shard_map/ppermute | solution.py:174
  265.6 24.9 %collective-permute-start.14 = (bf16[16,72,128]{2,1,0:T(8,128)(2,1)S(1)}, bf16[16,72,128]{2,1,0:T(8,128)(2,1)S(1)}, u32[]{:S(2)}, u32[]{:S(2)}) collective-permute-start(bf16[16,72,128]{2,1,0:T(8,128)(2,1)S(1)} %get-tuple-element.71), channel_id=1, source_target_pairs={{0,128},{64,192},{128,0},{192,64},{1,129},{65,193},{129,1},{193,65... | collective-permute-start | bytes 884744 | tf_op jit(solution)/shard_map/ppermute | solution.py:174
  265.6 24.9 %collective-permute-start.13 = (bf16[16,72,128]{2,1,0:T(8,128)(2,1)S(1)}, bf16[16,72,128]{2,1,0:T(8,128)(2,1)S(1)}, u32[]{:S(2)}, u32[]{:S(2)}) collective-permute-start(bf16[16,72,128]{2,1,0:T(8,128)(2,1)S(1)} %get-tuple-element.69), channel_id=1, source_target_pairs={{0,64},{64,0},{128,192},{192,128},{1,65},{65,1},{129,193},{193,129... | collective-permute-start | bytes 884744 | tf_op jit(solution)/shard_map/ppermute | solution.py:174
  (11 other events, 30.3 us)
Sparse Core Ops, SparseCore 0:
  56.2 47.6 all-gather.1
  217.4 49.5 reduce-scatter.1

commit v4 on v3

--- a/solution.py
+++ b/solution.py
@@ -94,30 +94,36 @@
     low = weight - high - middle
     facts = jnp.stack([slot.astype(F32), place.astype(F32), high, middle, low]).astype(BF16)
     facts = jnp.pad(facts, ((0, INFO - facts.shape[0]), (0, width - items)))
-    block = rows + INFO
 
     x_pieces, started = ring_steps(jnp.concatenate([tokens, facts], axis=0))
     all_g = lax.all_gather(after(cotangent, *started), ring, axis=0, tiled=True)
 
-    info = jnp.stack([p[rows : rows + 5, :items] for p in x_pieces]).astype(F32).reshape(NZ, 5, 2, rows)
-    source = ((jnp.arange(NZ, dtype=jnp.int32) + turn) % NZ)[:, None, None]
-    code = info[:, 0].astype(jnp.int32) - z_lo * PLANE
-    here = (code >= 0) & (code < PLANE)
-    code = jnp.where(here, (code * NZ + source) * CAP + info[:, 1].astype(jnp.int32), -1)
-    strength = info[:, 2] + info[:, 3] + info[:, 4]
     held = PLANE * NZ * CAP
     row_ids = jnp.arange(held, dtype=jnp.int32)[:, None]
 
     def flat(v):
         return jnp.moveaxis(v, 1, 0).reshape(2, -1)
 
+    def chosen(pieces, away):
+        info = jnp.stack([p[rows : rows + 5, :items] for p in pieces]).astype(F32).reshape(-1, 5, 2, rows)
+        source = ((jnp.array(away, jnp.int32) + turn) % NZ)[:, None, None]
+        code = info[:, 0].astype(jnp.int32) - z_lo * PLANE
+        here = (code >= 0) & (code < PLANE)
+        code = jnp.where(here, (code * NZ + source) * CAP + info[:, 1].astype(jnp.int32), -1)
+        code_x = flat(jnp.pad(code, ((0, 0), (0, 0), (0, INFO)), constant_values=-1))
+        pick_x = ((code_x[0][None, :] == row_ids) | (code_x[1][None, :] == row_ids)).astype(BF16)
+        pick_x = lax.optimization_barrier(pick_x)
+        return dot(pick_x, jnp.concatenate(pieces, axis=0), 1, 0), code, info[:, 2] + info[:, 3] + info[:, 4]
+
+    near, code_n, strength_n = chosen(x_pieces[:4] + x_pieces[5:], [0, 1, 2, 3, 5, 6, 7])
+    near = lax.optimization_barrier(near)
+    far, code_f, strength_f = chosen(x_pieces[4:5], [4])
+    code = jnp.concatenate([code_n[:4], code_f, code_n[4:]], axis=0)
+    strength = jnp.concatenate([strength_n[:4], strength_f, strength_n[4:]], axis=0)
+
     def from_zero(v):
         return flat(lax.dynamic_slice_in_dim(jnp.concatenate([v, v], axis=0), NZ - turn, NZ, axis=0))
 
-    code_x = flat(jnp.pad(code, ((0, 0), (0, 0), (0, INFO)), constant_values=-1))
-    pick_x = ((code_x[0][None, :] == row_ids) | (code_x[1][None, :] == row_ids)).astype(BF16)
-    pick_x, *x_pieces = lax.optimization_barrier((pick_x, *x_pieces))
-    all_x = jnp.concatenate(x_pieces, axis=0)
     code, strength = from_zero(code), from_zero(strength)
     first, second = code[0][None, :] == row_ids, code[1][None, :] == row_ids
     scale = jnp.sum(
@@ -138,7 +144,7 @@
         d_act = dot(g, w_down, 1, 1)
         return (d_act * for_gate).astype(BF16), (d_act * for_up).astype(BF16)
 
-    x = exchange(dot(pick_x, all_x, 1, 0).astype(BF16))
+    x = exchange((near + far).astype(BF16))
     sent_g = (dot(pick, all_g, 1, 0) * scale).astype(BF16)
     x, sent_g = lax.optimization_barrier((x, sent_g))
     x_o = swapped(x)

time: 300 us -> 303 us (1.010)
  waiting for transfers between devices: 144 us -> 134 us
  matrix products: 46.7 us -> 53.6 us
  local copies, waits for them, and re-layouts: 9.46 us -> 14.3 us
    ppermute x4, waiting for transfers between devices: 11.2 us -> 2.52 us  [ring_steps(): below.append(lax.ppermute(below[-1], ('zl', 'zh'), up))]
    dot_general x15 -> x16, matrix products: 46.7 us -> 53.6 us  [dot(): lax.dot_general(a, b, (((ca,), (cb,)), ((), ())), preferred_element_type=...]
    unnamed x40 -> x38, local copies, waits for them, and re-layouts: 4.73 us -> 10.1 us
    ppermute x3, waiting for transfers between devices: 27.8 us -> 22.6 us  [ring_steps(): above.append(lax.ppermute(above[-1], ('zl', 'zh'), down))]
    all_gather x1, waiting for transfers between devices: 18.6 us -> 22.8 us  [per_device(): all_g = lax.all_gather(after(cotangent, *started), ring, axis=0, tiled=True)]
  transfers between devices with their start and end apart: 22 -> 22, of which waited for: 15 -> 14; matrix products, arithmetic and copies ran while one was open for 15% -> 19% of each run, Pallas kernels for 0% -> 0%
where the time goes in v4:
time: 303 us; the launch traced here: 302 us
  waiting for transfers between devices  134 us (44%)
  starting transfers between devices  53.7 us (18%)
  matrix products  53.6 us (18%)
  blocking collectives  21.2 us (7%)
  between operations  14.4 us (5%)
  local copies, waits for them, and re-layouts  14.3 us (5%)
  other arithmetic  9.46 us (3%)
    dot_general x16, matrix products, dot(): lax.dot_general(a, b, (((ca,), (cb,)), ((), ())), preferred_element_type=...  53.6 us
    ppermute x6, waiting for transfers between devices, along_z(): lax.ppermute(piece, 'zl', [(z, z ^ d) for z in range(planes)])  45.9 us
    all_to_all x4, waiting for transfers between devices, exchange(): lax.all_to_all(chunks, ('y', 'x'), split_axis=0, concat_axis=0, tiled=True)  35 us
    all_to_all x4, starting transfers between devices, exchange(): lax.all_to_all(chunks, ('y', 'x'), split_axis=0, concat_axis=0, tiled=True)  30.8 us
    all_gather x1, waiting for transfers between devices, per_device(): all_g = lax.all_gather(after(cotangent, *started), ring, axis=0, tiled=True)  22.8 us
    ppermute x3, waiting for transfers between devices, ring_steps(): above.append(lax.ppermute(above[-1], ('zl', 'zh'), down))  22.6 us
    all_to_all x1, blocking collectives, exchange(): lax.all_to_all(chunks, ('y', 'x'), split_axis=0, concat_axis=0, tiled=True)  21.2 us
    ppermute x3, starting transfers between devices, ring_steps(): above.append(lax.ppermute(above[-1], ('zl', 'zh'), down))  13.4 us
  transfers between devices with their start and end apart: 22, of which 14 were waited for; matrix products, arithmetic and copies ran while one was open for 19% of the time, Pallas kernels for 0%

profile of v4, /device:TPU:2, one launch (start us, length us, event | category | flops | bytes accessed | tf_op | source)
XLA Modules:
  0.0 301.7 jit_solution(16069853764515682919)
XLA Ops:
  13.2 5.9 %collective-permute-start = (bf16[136,1792]{1,0:T(8,128)(2,1)S(1)}, bf16[136,1792]{1,0:T(8,128)(2,1)S(1)}, u32[]{:S(2)}, u32[]{:S(2)}) collective-permute-start(bf16[136,1792]{1,0:T(8,128)(2,1)S(1)} %pad_maximum_fusion.3), channel_id=1, source_target_pairs={{0,194},{64,0},{128,64},{192,128},{2,192},{66,2},{130,66},{194,130... | collective-permute-start | bytes 1462280 | tf_op jit(solution)/shard_map/ppermute | solution.py:75
  19.8 9.7 %collective-permute-done = bf16[136,1792]{1,0:T(8,128)(2,1)S(1)} collective-permute-done((bf16[136,1792]{1,0:T(8,128)(2,1)S(1)}, bf16[136,1792]{1,0:T(8,128)(2,1)S(1)}, u32[]{:S(2)}, u32[]{:S(2)}) %collective-permute-start) | collective-permute-done | bytes 487456 | tf_op jit(solution)/shard_map/ppermute | solution.py:75
  35.2 7.5 %collective-permute-done.1 = bf16[136,1792]{1,0:T(8,128)(2,1)} collective-permute-done((bf16[136,1792]{1,0:T(8,128)(2,1)S(1)}, bf16[136,1792]{1,0:T(8,128)(2,1)}, u32[]{:S(2)}, u32[]{:S(2)}) %collective-permute-start.1) | collective-permute-done | bytes 487456 | tf_op jit(solution)/shard_map/ppermute | solution.py:75
  42.7 3.8 %collective-permute-start.2 = (bf16[136,1792]{1,0:T(8,128)(2,1)}, bf16[136,1792]{1,0:T(8,128)(2,1)}, u32[]{:S(2)}, u32[]{:S(2)}) collective-permute-start(bf16[136,1792]{1,0:T(8,128)(2,1)} %collective-permute-done.1), channel_id=1, source_target_pairs={{0,194},{64,0},{128,64},{192,128},{2,192},{66,2},{130,66},{194,130... | collective-permute-start | bytes 1462280 | tf_op jit(solution)/shard_map/ppermute | solution.py:75
  50.0 5.4 %collective-permute-done.2 = bf16[136,1792]{1,0:T(8,128)(2,1)} collective-permute-done((bf16[136,1792]{1,0:T(8,128)(2,1)}, bf16[136,1792]{1,0:T(8,128)(2,1)}, u32[]{:S(2)}, u32[]{:S(2)}) %collective-permute-start.2) | collective-permute-done | bytes 487456 | tf_op jit(solution)/shard_map/ppermute | solution.py:75
  64.2 6.6 %fusion.52 = f32[640,1792]{1,0:T(8,128)} fusion(bf16[640,952]{1,0:T(8,128)(2,1)S(1)} %fusion.3, bf16[952,1792]{1,0:T(8,128)(2,1)} %constant_dynamic-update-slice_fusion.17), kind=kOutput, calls=%fused_computation.160 | convolution fusion | flops 2183659520 | bytes 9218048 | tf_op jit(solution)/shard_map/dot_general | solution.py:18
  71.2 4.5 %add_convert_fusion.2 = bf16[640,1792]{1,0:T(8,128)(2,1)} fusion(f32[640,1792]{1,0:T(8,128)} %fusion.52, bf16[640,136]{1,0:T(8,128)(2,1)S(1)} %fusion.31, bf16[136,1792]{1,0:T(8,128)(2,1)S(1)} %collective-permute-done.6), kind=kOutput, calls=%fused_computation.3 | convolution fusion | flops 314245120 | bytes 7542784 | tf_op jit(solution)/shard_map/dot_general | solution.py:18
  75.7 7.5 %all-to-all-start = ((bf16[16,40,1792]{2,1,0:T(8,128)(2,1)}), bf16[16,40,1792]{2,1,0:T(8,128)(2,1)}, u32[]{:S(2)}, u32[]{:S(2)}) async-start(bf16[16,40,1792]{2,1,0:T(8,128)(2,1)} %bitcast.23), calls=%async_computation | async-start | bytes 4587520 | tf_op jit(solution)/shard_map/all_to_all | solution.py:53
  84.0 22.8 %all-gather.2.cloned.1.call-done = bf16[1024,1792]{1,0:T(8,128)(2,1)} async-done(((bf16[128,1792]{1,0:T(8,128)(2,1)}), bf16[1024,1792]{1,0:T(8,128)(2,1)}) %all-gather.2.cloned.1.call-update) | async-done | bytes 3670032 | tf_op jit(solution)/shard_map/all_gather | solution.py:99
  106.8 6.3 %multiply_convert_fusion = bf16[640,1792]{1,0:T(8,128)(2,1)} fusion(bf16[1024,1792]{1,0:T(8,128)(2,1)} %all-gather.2.cloned.1.call-done, f32[640]{0:T(1024)S(1)} %add_reduce_fusion, s32[1024]{0:T(1024)S(1)} %bitcast.223, s32[1024]{0:T(1024)S(1)} %bitcast.220), kind=kOutput, calls=%fused_computation.2 | convolution fusion | flops 2353070080 | bytes 5974528 | tf_op jit(solution)/shard_map/dot_general | solution.py:18
  113.1 7.4 %all-to-all-start.1 = ((bf16[16,40,1792]{2,1,0:T(8,128)(2,1)}), bf16[16,40,1792]{2,1,0:T(8,128)(2,1)}, u32[]{:S(2)}, u32[]{:S(2)}) async-start(bf16[16,40,1792]{2,1,0:T(8,128)(2,1)} %bitcast.210), calls=%async_computation.1 | async-start | bytes 4587520 | tf_op jit(solution)/shard_map/all_to_all | solution.py:53
  123.3 3.9 %add_multiply_fusion.1 = (f32[640,320]{0,1:T(8,128)S(1)}, bf16[640,320]{0,1:T(8,128)(2,1)}, f32[640,320]{0,1:T(8,128)}) fusion(f32[640,320]{0,1:T(8,128)S(1)} %fusion.18, bf16[640,1792]{1,0:T(8,128)(2,1)} %bitcast.24, bf16[1,1792,320]{1,2,0:T(8,128)(2,1)S(1)} %copy-done), kind=kOutput, calls=%fused_computation.48 | convolution fusion | flops 736256000 | bytes 6307840 | tf_op jit(solution)/shard_map/dot_general | solution.py:18
  129.9 4.2 %add_multiply_fusion = (f32[640,320]{0,1:T(8,128)}, bf16[640,320]{0,1:T(8,128)(2,1)}, f32[640,320]{0,1:T(8,128)}) fusion(f32[640,320]{0,1:T(8,128)S(1)} %fusion.16, bf16[640,1792]{1,0:T(8,128)(2,1)} %collective-permute-done.7, bf16[1,1792,320]{1,2,0:T(8,128)(2,1)S(1)} %copy-done), kind=kOutput, calls=%fused_computation.44 | convolution fusion | flops 736256000 | bytes 6307840 | tf_op jit(solution)/shard_map/dot_general | solution.py:18
  134.1 18.8 %all-to-all-done.1 = bf16[16,40,1792]{2,1,0:T(8,128)(2,1)} async-done(((bf16[16,40,1792]{2,1,0:T(8,128)(2,1)}), bf16[16,40,1792]{2,1,0:T(8,128)(2,1)}, u32[]{:S(2)}, u32[]{:S(2)}) %all-to-all-start.1) | async-done | bytes 2293792 | tf_op jit(solution)/shard_map/all_to_all | solution.py:53
  152.8 4.6 %collective-permute-done.8 = bf16[640,1792]{1,0:T(8,128)(2,1)S(1)} collective-permute-done((bf16[640,1792]{1,0:T(8,128)(2,1)}, bf16[640,1792]{1,0:T(8,128)(2,1)S(1)}, u32[]{:S(2)}, u32[]{:S(2)}) %collective-permute-start.8) | collective-permute-done | bytes 2293792 | tf_op jit(solution)/shard_map/ppermute | solution.py:58
  172.0 8.6 %all-to-all-start.2 = ((bf16[16,40,1792]{2,1,0:T(8,128)(2,1)}), bf16[16,40,1792]{2,1,0:T(8,128)(2,1)S(1)}, u32[]{:S(2)}, u32[]{:S(2)}) async-start(bf16[16,40,1792]{2,1,0:T(8,128)(2,1)} %bitcast.36), calls=%async_computation.2 | async-start | bytes 4587520 | tf_op jit(solution)/shard_map/all_to_all | solution.py:53
  191.0 7.4 %collective-permute-done.12 = bf16[16,72,128]{2,1,0:T(8,128)(2,1)S(1)} collective-permute-done((bf16[16,72,128]{2,1,0:T(8,128)(2,1)S(1)}, bf16[16,72,128]{2,1,0:T(8,128)(2,1)S(1)}, u32[]{:S(2)}, u32[]{:S(2)}) %collective-permute-start.12) | collective-permute-done | bytes 294944 | tf_op jit(solution)/shard_map/ppermute | solution.py:180
  198.4 15.3 %collective-permute-done.11 = bf16[16,72,128]{2,1,0:T(8,128)(2,1)S(1)} collective-permute-done((bf16[16,72,128]{2,1,0:T(8,128)(2,1)S(1)}, bf16[16,72,128]{2,1,0:T(8,128)(2,1)S(1)}, u32[]{:S(2)}, u32[]{:S(2)}) %collective-permute-start.11) | collective-permute-done | bytes 294944 | tf_op jit(solution)/shard_map/ppermute | solution.py:180
  215.0 4.5 %convolution_convert_fusion = bf16[1024,1792]{1,0:T(8,128)(2,1)} fusion(bf16[640,1792]{1,0:T(8,128)(2,1)S(1)} %bitcast.209, s32[1024]{0:T(1024)S(1)} %bitcast.224, s32[1024]{0:T(1024)S(1)} %bitcast.221), kind=kOutput, calls=%fused_computation.4 | convolution fusion | flops 2352611328 | bytes 5971968 | tf_op jit(solution)/shard_map/dot_general | solution.py:18
  219.5 7.3 %all-to-all-start.3 = ((bf16[16,1,4,72,128]{4,3,2,1,0:T(8,128)(2,1)}), bf16[16,1,4,72,128]{4,3,2,1,0:T(8,128)(2,1)S(1)}, u32[]{:S(2)}, u32[]{:S(2)}) async-start(bf16[16,1,4,72,128]{4,3,2,1,0:T(8,128)(2,1)} %bitcast.49), calls=%async_computation.4 | async-start | bytes 2359296 | tf_op jit(solution)/shard_map/all_to_all | solution.py:53
  226.9 16.2 %all-to-all-done.3 = bf16[16,1,4,72,128]{4,3,2,1,0:T(8,128)(2,1)S(1)} async-done(((bf16[16,1,4,72,128]{4,3,2,1,0:T(8,128)(2,1)}), bf16[16,1,4,72,128]{4,3,2,1,0:T(8,128)(2,1)S(1)}, u32[]{:S(2)}, u32[]{:S(2)}) %all-to-all-start.3) | async-done | bytes 1179680 | tf_op jit(solution)/shard_map/all_to_all | solution.py:53
  244.4 21.2 %all_to_all.25 = bf16[16,1,4,72,128]{4,3,2,1,0:T(8,128)(2,1)S(1)} all-to-all(bf16[16,1,4,72,128]{4,3,2,1,0:T(8,128)(2,1)S(1)} %bitcast.205), channel_id=1, replica_groups=mesh['zl'=4,'y'=4,'x'=4,'zh'=2,'c'=2] {'y','x'}, dimensions={0} | all-to-all | bytes 2359296 | tf_op jit(solution)/shard_map/all_to_all | solution.py:53
  270.2 7.4 %collective-permute-done.15 = bf16[16,72,128]{2,1,0:T(8,128)(2,1)S(1)} collective-permute-done((bf16[16,72,128]{2,1,0:T(8,128)(2,1)S(1)}, bf16[16,72,128]{2,1,0:T(8,128)(2,1)S(1)}, u32[]{:S(2)}, u32[]{:S(2)}) %collective-permute-start.15) | collective-permute-done | bytes 294944 | tf_op jit(solution)/shard_map/ppermute | solution.py:180
  277.6 15.7 %collective-permute-done.14 = bf16[16,72,128]{2,1,0:T(8,128)(2,1)S(1)} collective-permute-done((bf16[16,72,128]{2,1,0:T(8,128)(2,1)S(1)}, bf16[16,72,128]{2,1,0:T(8,128)(2,1)S(1)}, u32[]{:S(2)}, u32[]{:S(2)}) %collective-permute-start.14) | collective-permute-done | bytes 294944 | tf_op jit(solution)/shard_map/ppermute | solution.py:180
  (136 shorter events, 64.5 us)
Async XLA Ops:
  7.2 116.1 %copy-start = (bf16[1,1792,320]{1,2,0:T(8,128)(2,1)S(1)}, bf16[1,1792,320]{1,2,0:T(8,128)(2,1)}, u32[]{:S(2)}) copy-start(bf16[1,1792,320]{1,2,0:T(8,128)(2,1)} %param.15) | copy-start | bytes 3440644
  7.2 99.6 %all-gather.2.cloned.1.call-start = ((), (), s32[]{:S(2)}) async-start(), calls=%async_computation.6 | async-start | bytes 4128768 | tf_op jit(solution)/shard_map/all_gather | solution.py:99
  13.2 16.3 %collective-permute-start = (bf16[136,1792]{1,0:T(8,128)(2,1)S(1)}, bf16[136,1792]{1,0:T(8,128)(2,1)S(1)}, u32[]{:S(2)}, u32[]{:S(2)}) collective-permute-start(bf16[136,1792]{1,0:T(8,128)(2,1)S(1)} %pad_maximum_fusion.3), channel_id=1, source_target_pairs={{0,194},{64,0},{128,64},{192,128},{2,192},{66,2},{130,66},{194,130... | collective-permute-start | bytes 1462280 | tf_op jit(solution)/shard_map/ppermute | solution.py:75
  19.1 14.1 %collective-permute-start.3 = (bf16[136,1792]{1,0:T(8,128)(2,1)S(1)}, bf16[136,1792]{1,0:T(8,128)(2,1)S(1)}, u32[]{:S(2)}, u32[]{:S(2)}) collective-permute-start(bf16[136,1792]{1,0:T(8,128)(2,1)S(1)} %pad_maximum_fusion.3), channel_id=1, source_target_pairs={{0,64},{64,128},{128,192},{192,2},{2,66},{66,130},{130,194},{194,0... | collective-permute-start | bytes 1462280 | tf_op jit(solution)/shard_map/ppermute | solution.py:73
  29.5 13.2 %collective-permute-start.1 = (bf16[136,1792]{1,0:T(8,128)(2,1)S(1)}, bf16[136,1792]{1,0:T(8,128)(2,1)}, u32[]{:S(2)}, u32[]{:S(2)}) collective-permute-start(bf16[136,1792]{1,0:T(8,128)(2,1)S(1)} %collective-permute-done), channel_id=1, source_target_pairs={{0,194},{64,0},{128,64},{192,128},{2,192},{66,2},{130,66},{194,130... | collective-permute-start | bytes 1462280 | tf_op jit(solution)/shard_map/ppermute | solution.py:75
  33.2 13.3 %collective-permute-start.4 = (bf16[136,1792]{1,0:T(8,128)(2,1)S(1)}, bf16[136,1792]{1,0:T(8,128)(2,1)S(1)}, u32[]{:S(2)}, u32[]{:S(2)}) collective-permute-start(bf16[136,1792]{1,0:T(8,128)(2,1)S(1)} %collective-permute-done.3), channel_id=1, source_target_pairs={{0,64},{64,128},{128,192},{192,2},{2,66},{66,130},{130,194},{194,0... | collective-permute-start | bytes 1462280 | tf_op jit(solution)/shard_map/ppermute | solution.py:73
  42.7 12.7 %collective-permute-start.2 = (bf16[136,1792]{1,0:T(8,128)(2,1)}, bf16[136,1792]{1,0:T(8,128)(2,1)}, u32[]{:S(2)}, u32[]{:S(2)}) collective-permute-start(bf16[136,1792]{1,0:T(8,128)(2,1)} %collective-permute-done.1), channel_id=1, source_target_pairs={{0,194},{64,0},{128,64},{192,128},{2,192},{66,2},{130,66},{194,130... | collective-permute-start | bytes 1462280 | tf_op jit(solution)/shard_map/ppermute | solution.py:75
  46.5 12.0 %collective-permute-start.5 = (bf16[136,1792]{1,0:T(8,128)(2,1)S(1)}, bf16[136,1792]{1,0:T(8,128)(2,1)S(1)}, u32[]{:S(2)}, u32[]{:S(2)}) collective-permute-start(bf16[136,1792]{1,0:T(8,128)(2,1)S(1)} %collective-permute-done.4), channel_id=1, source_target_pairs={{0,64},{64,128},{128,192},{192,2},{2,66},{66,130},{130,194},{194,0... | collective-permute-start | bytes 1462280 | tf_op jit(solution)/shard_map/ppermute | solution.py:73
  59.8 11.2 %collective-permute-start.6 = (bf16[136,1792]{1,0:T(8,128)(2,1)S(1)}, bf16[136,1792]{1,0:T(8,128)(2,1)S(1)}, u32[]{:S(2)}, u32[]{:S(2)}) collective-permute-start(bf16[136,1792]{1,0:T(8,128)(2,1)S(1)} %collective-permute-done.5), channel_id=1, source_target_pairs={{0,64},{64,128},{128,192},{192,2},{2,66},{66,130},{130,194},{194,0... | collective-permute-start | bytes 1462280 | tf_op jit(solution)/shard_map/ppermute | solution.py:73
  75.7 37.4 %all-to-all-start = ((bf16[16,40,1792]{2,1,0:T(8,128)(2,1)}), bf16[16,40,1792]{2,1,0:T(8,128)(2,1)}, u32[]{:S(2)}, u32[]{:S(2)}) async-start(bf16[16,40,1792]{2,1,0:T(8,128)(2,1)} %bitcast.23), calls=%async_computation | async-start | bytes 4587520 | tf_op jit(solution)/shard_map/all_to_all | solution.py:53
  113.1 14.1 %collective-permute-start.7 = (bf16[640,1792]{1,0:T(8,128)(2,1)}, bf16[640,1792]{1,0:T(8,128)(2,1)}, u32[]{:S(2)}, u32[]{:S(2)}) collective-permute-start(bf16[640,1792]{1,0:T(8,128)(2,1)} %bitcast.24), channel_id=1, source_target_pairs={{0,1},{1,0},{2,3},{3,2},{4,5},{5,4},{6,7},{7,6},{8,9},{9,8},{10,11... | collective-permute-start | bytes 6881288 | tf_op jit(solution)/shard_map/ppermute | solution.py:58
  113.1 39.7 %all-to-all-start.1 = ((bf16[16,40,1792]{2,1,0:T(8,128)(2,1)}), bf16[16,40,1792]{2,1,0:T(8,128)(2,1)}, u32[]{:S(2)}, u32[]{:S(2)}) async-start(bf16[16,40,1792]{2,1,0:T(8,128)(2,1)} %bitcast.210), calls=%async_computation.1 | async-start | bytes 4587520 | tf_op jit(solution)/shard_map/all_to_all | solution.py:53
  152.8 8.4 %copy-start.3 = (f32[640,320]{0,1:T(8,128)S(1)}, f32[640,320]{0,1:T(8,128)}, u32[]{:S(2)}) copy-start(f32[640,320]{0,1:T(8,128)} %get-tuple-element.25) | copy-start | bytes 2457604
  152.8 4.7 %collective-permute-start.8 = (bf16[640,1792]{1,0:T(8,128)(2,1)}, bf16[640,1792]{1,0:T(8,128)(2,1)S(1)}, u32[]{:S(2)}, u32[]{:S(2)}) collective-permute-start(bf16[640,1792]{1,0:T(8,128)(2,1)} %bitcast.34), channel_id=1, source_target_pairs={{0,1},{1,0},{2,3},{3,2},{4,5},{5,4},{6,7},{7,6},{8,9},{9,8},{10,11... | collective-permute-start | bytes 6881288 | tf_op jit(solution)/shard_map/ppermute | solution.py:58
  164.2 4.7 %collective-permute-start.9 = (bf16[640,1792]{1,0:T(8,128)(2,1)S(1)}, bf16[640,1792]{1,0:T(8,128)(2,1)S(1)}, u32[]{:S(2)}, u32[]{:S(2)}) collective-permute-start(bf16[640,1792]{1,0:T(8,128)(2,1)S(1)} %add_convert_fusion.1), channel_id=1, source_target_pairs={{0,1},{1,0},{2,3},{3,2},{4,5},{5,4},{6,7},{7,6},{8,9},{9,8},{10,11... | collective-permute-start | bytes 6881288 | tf_op jit(solution)/shard_map/ppermute | solution.py:58
  172.0 42.9 %all-to-all-start.2 = ((bf16[16,40,1792]{2,1,0:T(8,128)(2,1)}), bf16[16,40,1792]{2,1,0:T(8,128)(2,1)S(1)}, u32[]{:S(2)}, u32[]{:S(2)}) async-start(bf16[16,40,1792]{2,1,0:T(8,128)(2,1)} %bitcast.36), calls=%async_computation.2 | async-start | bytes 4587520 | tf_op jit(solution)/shard_map/all_to_all | solution.py:53
  180.6 114.2 %reduce-scatter.2.cloned.1.call-start = ((), (), s32[]{:S(2)}) async-start(), calls=%async_computation.7 | async-start | bytes 4128768 | tf_op jit(solution)/shard_map/reduce_scatter | solution.py:188
  186.5 11.9 %collective-permute-start.12 = (bf16[16,72,128]{2,1,0:T(8,128)(2,1)S(1)}, bf16[16,72,128]{2,1,0:T(8,128)(2,1)S(1)}, u32[]{:S(2)}, u32[]{:S(2)}) collective-permute-start(bf16[16,72,128]{2,1,0:T(8,128)(2,1)S(1)} %get-tuple-element.57), channel_id=1, source_target_pairs={{0,192},{64,128},{128,64},{192,0},{1,193},{65,129},{129,65},{193,1... | collective-permute-start | bytes 884744 | tf_op jit(solution)/shard_map/ppermute | solution.py:180
  189.6 24.2 %collective-permute-start.11 = (bf16[16,72,128]{2,1,0:T(8,128)(2,1)S(1)}, bf16[16,72,128]{2,1,0:T(8,128)(2,1)S(1)}, u32[]{:S(2)}, u32[]{:S(2)}) collective-permute-start(bf16[16,72,128]{2,1,0:T(8,128)(2,1)S(1)} %get-tuple-element.58), channel_id=1, source_target_pairs={{0,128},{64,192},{128,0},{192,64},{1,129},{65,193},{129,1},{193,65... | collective-permute-start | bytes 884744 | tf_op jit(solution)/shard_map/ppermute | solution.py:180
  189.6 24.2 %collective-permute-start.10 = (bf16[16,72,128]{2,1,0:T(8,128)(2,1)S(1)}, bf16[16,72,128]{2,1,0:T(8,128)(2,1)S(1)}, u32[]{:S(2)}, u32[]{:S(2)}) collective-permute-start(bf16[16,72,128]{2,1,0:T(8,128)(2,1)S(1)} %get-tuple-element.59), channel_id=1, source_target_pairs={{0,64},{64,0},{128,192},{192,128},{1,65},{65,1},{129,193},{193,129... | collective-permute-start | bytes 884744 | tf_op jit(solution)/shard_map/ppermute | solution.py:180
  219.5 23.6 %all-to-all-start.3 = ((bf16[16,1,4,72,128]{4,3,2,1,0:T(8,128)(2,1)}), bf16[16,1,4,72,128]{4,3,2,1,0:T(8,128)(2,1)S(1)}, u32[]{:S(2)}, u32[]{:S(2)}) async-start(bf16[16,1,4,72,128]{4,3,2,1,0:T(8,128)(2,1)} %bitcast.49), calls=%async_computation.4 | async-start | bytes 2359296 | tf_op jit(solution)/shard_map/all_to_all | solution.py:53
  265.7 11.9 %collective-permute-start.15 = (bf16[16,72,128]{2,1,0:T(8,128)(2,1)S(1)}, bf16[16,72,128]{2,1,0:T(8,128)(2,1)S(1)}, u32[]{:S(2)}, u32[]{:S(2)}) collective-permute-start(bf16[16,72,128]{2,1,0:T(8,128)(2,1)S(1)} %get-tuple-element.54), channel_id=1, source_target_pairs={{0,192},{64,128},{128,64},{192,0},{1,193},{65,129},{129,65},{193,1... | collective-permute-start | bytes 884744 | tf_op jit(solution)/shard_map/ppermute | solution.py:180
  268.4 24.9 %collective-permute-start.14 = (bf16[16,72,128]{2,1,0:T(8,128)(2,1)S(1)}, bf16[16,72,128]{2,1,0:T(8,128)(2,1)S(1)}, u32[]{:S(2)}, u32[]{:S(2)}) collective-permute-start(bf16[16,72,128]{2,1,0:T(8,128)(2,1)S(1)} %get-tuple-element.55), channel_id=1, source_target_pairs={{0,128},{64,192},{128,0},{192,64},{1,129},{65,193},{129,1},{193,65... | collective-permute-start | bytes 884744 | tf_op jit(solution)/shard_map/ppermute | solution.py:180
  268.4 24.9 %collective-permute-start.13 = (bf16[16,72,128]{2,1,0:T(8,128)(2,1)S(1)}, bf16[16,72,128]{2,1,0:T(8,128)(2,1)S(1)}, u32[]{:S(2)}, u32[]{:S(2)}) collective-permute-start(bf16[16,72,128]{2,1,0:T(8,128)(2,1)S(1)} %get-tuple-element.53), channel_id=1, source_target_pairs={{0,64},{64,0},{128,192},{192,128},{1,65},{65,1},{129,193},{193,129... | collective-permute-start | bytes 884744 | tf_op jit(solution)/shard_map/ppermute | solution.py:180
  (7 other events, 24.0 us)
Sparse Core Ops, SparseCore 0:
  59.1 47.6 all-gather.1
  219.6 50.1 reduce-scatter.1
